TPU v7x, 128 devices: a whole 4x4x4 slice. The times are simulated.
128 devices in a mesh: blk: 16 (over y, z), grp: 8 (over x, core).
Axes of the slice: x: 4, y: 4, z: 4, core: 2. Of those that a mesh axis runs over, the one named last changes fastest.
Arguments:
- image_embed: bfloat16 [16384, 1280], P(('blk', 'grp')), may hold values from -0.8 to 0.8
- text_embed: bfloat16 [16384, 1280], P(('blk', 'grp')), may hold values from -0.8 to 0.8
- log_scale: float32 [1], replicated, may hold values from 4 to 4.6
- pairing: int32 [16], replicated, may hold values from 0 to 15, as said below
Outputs:
- grad_image: float32 [16384, 1280], P(('blk', 'grp'))
- grad_text: float32 [16384, 1280], P(('blk', 'grp'))
- loss: float32 [1], replicated
- grad_log_scale: float32 [1], replicated
Inputs may be any that keep to these rules, and one draw needn't show every extreme that they name: pairing holds each of the 16 block numbers once: the matching caption of image row r is text row pairing[r // 1024] * 1024 + r % 1024.
All inputs are finite; a program needn't handle non-finite values.
Results may differ from a plain program's by a relative error of at most 0.015.
Values may be sent and summed in bfloat16 or wider, within the bound.
A program may use at most 64 MiB of HBM per device.

v0:
```python
import jax
import jax.numpy as jnp
from jax import lax
from jax.sharding import PartitionSpec as P

softcap = 30.0


def normalize(embed):
    wide = embed.astype(jnp.float32)
    inverse = lax.rsqrt(jnp.sum(wide * wide, axis=1, keepdims=True) + 1e-06)
    unit = wide * inverse
    return (inverse, unit, unit.astype(jnp.bfloat16))


def back_norm(inverse, unit, grad_unit):
    inner = jnp.sum(unit * grad_unit, axis=1, keepdims=True)
    return inverse * (grad_unit - unit * inner)


def local(image_embed, text_embed, log_scale, pairing):
    img_inverse, img_unit, img_norm = normalize(image_embed)
    txt_inverse, txt_unit, txt_norm = normalize(text_embed)
    scale = jnp.exp(log_scale[0])
    shard_rows = image_embed.shape[0]
    blk_count = lax.axis_size("blk")
    batch_rows = shard_rows * lax.axis_size("grp") * blk_count
    blk_index = lax.axis_index("blk")
    grp_index = lax.axis_index("grp")
    offset = (pairing[blk_index] - grp_index) * shard_rows
    lower = grp_index * shard_rows
    block_rows = lax.all_gather(img_norm, "grp", axis=0, tiled=True)
    block_count = block_rows.shape[0]

    def tile(piece):
        cosine = lax.dot_general(
            block_rows, piece, (((1,), (1,)), ((), ())), preferred_element_type=jnp.float32
        )
        capped = softcap * jnp.tanh(scale * cosine / softcap)
        count = piece.shape[0]
        row_ids = lax.broadcasted_iota(jnp.int32, (block_count, count), 0)
        col_ids = lax.broadcasted_iota(jnp.int32, (block_count, count), 1)
        inside = (row_ids >= lower) & (row_ids < lower + shard_rows)
        partner = ((col_ids == row_ids + offset) & inside).astype(jnp.float32)
        return (cosine, capped, partner)

    cosine, capped, partner = tile(lax.all_gather(txt_norm, "blk", axis=0, tiled=True))
    powers = jnp.exp(capped)
    row_sum = jnp.sum(powers, axis=1)
    col_sum = jnp.sum(powers, axis=0)
    row_sum, col_sum, positive = (row_sum, col_sum, jnp.sum(capped * partner))
    row_lse = jnp.log(lax.psum(row_sum, "grp"))
    col_lse = jnp.log(lax.psum(col_sum, "blk"))
    row_own = lax.dynamic_slice_in_dim(row_lse, lower, shard_rows, 0)
    col_own = lax.dynamic_slice_in_dim(col_lse, blk_index * shard_rows, shard_rows, 0)
    loss_part = jnp.sum(row_own) + jnp.sum(col_own) - 2.0 * positive
    piece = lax.all_gather(txt_norm, "blk", axis=0, tiled=True)
    count = piece.shape[0]
    cosine, capped, partner = tile(piece)
    weight = (
        0.5 * (jnp.exp(capped - row_lse[:, None]) + jnp.exp(capped - col_lse[None, :])) - partner
    )
    ratio = capped / softcap
    slope_term = weight * (1.0 - ratio * ratio)
    grad_logit = (scale * slope_term).astype(jnp.bfloat16)
    grad_rows = jnp.dot(grad_logit, piece, preferred_element_type=jnp.float32)
    columns = lax.dot_general(
        grad_logit, block_rows, (((0,), (0,)), ((), ())), preferred_element_type=jnp.float32
    )
    grad_cols = columns
    grad_rows, grad_cols, slope = (grad_rows, grad_cols, jnp.sum(slope_term * cosine))
    grad_img_unit = lax.psum_scatter(
        grad_rows.astype(jnp.bfloat16), "grp", scatter_dimension=0, tiled=True
    ).astype(jnp.float32)
    grad_txt_unit = lax.psum_scatter(
        grad_cols.astype(jnp.bfloat16), "blk", scatter_dimension=0, tiled=True
    ).astype(jnp.float32)
    totals = lax.psum((loss_part, slope), ("blk", "grp"))
    loss = totals[0] / (2.0 * batch_rows)
    grad_log_scale = scale * totals[1] / batch_rows
    grad_image = back_norm(img_inverse, img_unit, grad_img_unit)
    grad_text = back_norm(txt_inverse, txt_unit, grad_txt_unit)
    return (grad_image, grad_text, jnp.reshape(loss, (1,)), jnp.reshape(grad_log_scale, (1,)))


def solution(mesh):
    return jax.shard_map(
        local,
        mesh=mesh,
        in_specs=(P(("blk", "grp"), None), P(("blk", "grp"), None), P(), P()),
        out_specs=(P(("blk", "grp"), None), P(("blk", "grp"), None), P(), P()),
        check_vma=False,
    )
```

profile of v0, /device:TPU:1, one launch (start us, length us, event | category | flops | bytes accessed | tf_op | source)
XLA Modules:
  0.0 301.5 jit_solution(16702936613546125250)
XLA Ops:
  7.2 1.1 fusion.7
  8.3 1.8 fusion.6
  10.2 0.0 all-gather.5.cloned.1.call-start
  10.2 1.1 fusion.8
  11.4 1.8 fusion.4
  13.2 0.0 reduce-scatter.3.cloned.1.call-start
  14.0 1.2 dynamic_slice.9
  15.9 24.2 %all-gather.3.cloned.1.call-done = bf16[1024,1280]{1,0:T(8,128)(2,1)} async-done(((bf16[128,1280]{1,0:T(8,128)(2,1)}), bf16[1024,1280]{1,0:T(8,128)(2,1)}) %all-gather.3.cloned.1.call-update) | async-done | bytes 2621456 | tf_op jit(solution)/shard_map/all_gather | solution.py:32
  40.1 59.4 %all-gather.5.cloned.1.call-done = bf16[2048,1280]{1,0:T(8,128)(2,1)} async-done(((bf16[128,1280]{1,0:T(8,128)(2,1)}), bf16[2048,1280]{1,0:T(8,128)(2,1)}) %all-gather.5.cloned.1.call-update) | async-done | bytes 5242896 | tf_op jit(solution)/shard_map/all_gather | solution.py:57
  99.5 11.8 %fusion.2 = (f32[1024]{0:T(1024)S(1)}, f32[2048]{0:T(1024)S(1)}, f32[1024,2048]{1,0:T(8,128)}) fusion(f32[]{:T(128)} %bitcast, bf16[1024,1280]{1,0:T(8,128)(2,1)} %all-gather.3.cloned.1.call-done, bf16[2048,1280]{1,0:T(8,128)(2,1)} %all-gather.5.cloned.1.call-done), kind=kOutput, calls=%fused_computation.10 | convolution fusion | flops 5379191808 | bytes 16265220 | tf_op jit(solution)/shard_map/dot_general | solution.py:36
  111.3 12.4 %psum.28 = f32[1024]{0:T(1024)S(1)} all-reduce(f32[1024]{0:T(1024)S(1)} %get-tuple-element.6), channel_id=1, replica_groups=mesh['blk'=16,'grp'=8] {'grp'}, use_global_device_ids=true, to_apply=%region_3.0 | all-reduce | flops 1024 | bytes 8192 | tf_op jit(solution)/shard_map/psum | solution.py:52
  123.8 31.9 %psum.29 = f32[2048]{0:T(1024)S(1)} all-reduce(f32[2048]{0:T(1024)S(1)} %get-tuple-element.7), channel_id=1, replica_groups=mesh['blk'=16,'grp'=8] {'blk'}, use_global_device_ids=true, to_apply=%region_5.0 | all-reduce | flops 2048 | bytes 16384 | tf_op jit(solution)/shard_map/psum | solution.py:53
  155.7 15.9 %convolution_convert_fusion.1 = bf16[1024,1280]{1,0:T(8,128)(2,1)} fusion(bf16[2048,1280]{1,0:T(8,128)(2,1)} %all-gather.5.cloned.1.call-done, f32[]{:T(128)} %bitcast, s32[1024]{0:T(1024)S(1)} %iota_add_fusion, f32[2048]{0:T(1024)S(1)} %log.7, f32[1024]{0:T(1024)S(1)} %log.6, pred[1024]{0:T(1024)(128)(4,1)S(1)} %fusion.13, f32[1024,2048]{1,0:T(8,128)} %get-tuple-element.10), kind=kOutput, calls=%fused_computation.11 | convolution fusion | flops 5403574272 | bytes 16270340 | tf_op jit(solution)/shard_map/dot_general | solution.py:66
  171.6 0.2 reduce-scatter.5.cloned.1.call-start
  171.9 14.4 %convolution_convert_fusion = bf16[2048,1280]{1,0:T(8,128)(2,1)} fusion(bf16[1024,1280]{1,0:T(8,128)(2,1)S(1)} %copy-done.2, f32[]{:T(128)} %bitcast, s32[1024]{0:T(1024)S(1)} %iota_add_fusion, f32[2048]{0:T(1024)S(1)} %log.7, f32[1024]{0:T(1024)S(1)} %log.6, pred[1024]{0:T(1024)(128)(4,1)S(1)} %fusion.13, f32[1024,2048]{1,0:T(8,128)} %get-tuple-element.10), kind=kOutput, calls=%fused_computation.8 | convolution fusion | flops 5404884992 | bytes 16270340 | tf_op jit(solution)/shard_map/dot_general | solution.py:67
  186.3 0.7 dynamic-slice_reduce_fusion.1
  187.0 0.7 dynamic-slice_reduce_fusion
  189.0 10.0 %multiply_reduce_fusion = (f32[]{:T(128)}, f32[]{:T(128)}) fusion(f32[1024,2048]{1,0:T(8,128)} %get-tuple-element.10, pred[1024]{0:T(1024)(128)(4,1)S(1)} %fusion.13, s32[1024]{0:T(1024)S(1)} %iota_add_fusion, f32[2048]{0:T(1024)S(1)} %log.7, f32[1024]{0:T(1024)S(1)} %log.6, f32[]{:T(128)} %bitcast), kind=kLoop, calls=%fused_computation | loop fusion | flops 37748736 | bytes 8406028 | tf_op jit(solution)/shard_map/reduce_sum | solution.py:71
  199.6 71.9 %all-reduce = (f32[]{:T(128)}, f32[]{:T(128)}) all-reduce(f32[]{:T(128)S(6)} %sub.47, f32[]{:T(128)} %get-tuple-element.4), channel_id=1, replica_groups=mesh['blk'=16,'grp'=8] {'blk','grp'}, use_global_device_ids=true, to_apply=%region_13.0 | all-reduce | flops 2 | bytes 16 | tf_op jit(solution)/shard_map/psum | solution.py:78
  272.9 1.2 fusion.9
  274.1 2.1 fusion.10
  276.2 13.2 %reduce-scatter.5.cloned.1.call-done = bf16[128,1280]{1,0:T(8,128)(2,1)} async-done(((bf16[2048,1280]{1,0:T(8,128)(2,1)}), bf16[128,1280]{1,0:T(8,128)(2,1)}) %reduce-scatter.5.cloned.1.call-update) | async-done | bytes 327696 | tf_op jit(solution)/shard_map/reduce_scatter | solution.py:75
  289.4 1.2 fusion.11
  290.6 2.1 fusion.12
  (18 shorter events, 0.2 us)
Async XLA Ops:
  7.2 32.9 %all-gather.3.cloned.1.call-start = ((), (), s32[]{:S(2)}) async-start(), calls=%async_computation.2 | async-start | bytes 2949120 | tf_op jit(solution)/shard_map/all_gather | solution.py:32
  10.2 89.3 %all-gather.5.cloned.1.call-start = ((), (), s32[]{:S(2)}) async-start(), calls=%async_computation.3 | async-start | bytes 5570560 | tf_op jit(solution)/shard_map/all_gather | solution.py:57
  13.2 259.6 %reduce-scatter.3.cloned.1.call-start = ((), (), s32[]{:S(2)}) async-start(), calls=%async_computation.4 | async-start | bytes 2949120 | tf_op jit(solution)/shard_map/reduce_scatter | solution.py:72
  155.6 16.2 %copy-start.2 = (bf16[1024,1280]{1,0:T(8,128)(2,1)S(1)}, bf16[1024,1280]{1,0:T(8,128)(2,1)}, u32[]{:S(2)}) copy-start(bf16[1024,1280]{1,0:T(8,128)(2,1)} %all-gather.3.cloned.1.call-done) | copy-start | bytes 7864324
  171.6 117.8 %reduce-scatter.5.cloned.1.call-start = ((), (), s32[]{:S(2)}) async-start(), calls=%async_computation.5 | async-start | bytes 5570560 | tf_op jit(solution)/shard_map/reduce_scatter | solution.py:75
  186.3 86.5 %copy-start = (bf16[128,1280]{1,0:T(8,128)(2,1)S(1)}, bf16[128,1280]{1,0:T(8,128)(2,1)}, u32[]{:S(2)}) copy-start(bf16[128,1280]{1,0:T(8,128)(2,1)} %param.4) | copy-start | bytes 983044
  186.3 103.1 %copy-start.1 = (bf16[128,1280]{1,0:T(8,128)(2,1)S(1)}, bf16[128,1280]{1,0:T(8,128)(2,1)}, u32[]{:S(2)}) copy-start(bf16[128,1280]{1,0:T(8,128)(2,1)} %param.5) | copy-start | bytes 983044
Sparse Core Ops, SparseCore 0:
  10.3 29.7 all-gather.2
  42.8 56.6 all-gather.4
  171.7 34.2 reduce-scatter.2
  209.3 80.0 reduce-scatter.4
where the time goes:
time: 302 us; the launch traced here: 301 us
  blocking collectives  116 us (38%)
  waiting for transfers between devices  96.9 us (32%)
  matrix products  42.2 us (14%)
  other arithmetic  23.9 us (8%)
  between operations  20.7 us (7%)
    psum x1, blocking collectives, local(): totals = lax.psum((loss_part, slope), ('blk', 'grp'))  71.9 us
    all_gather x1, waiting for transfers between devices, local(): piece = lax.all_gather(txt_norm, 'blk', axis=0, tiled=True)  59.4 us
    psum x1, blocking collectives, local(): col_lse = jnp.log(lax.psum(col_sum, 'blk'))  31.9 us
    all_gather x1, waiting for transfers between devices, local(): block_rows = lax.all_gather(img_norm, 'grp', axis=0, tiled=True)  24.2 us
    dot_general x1, matrix products, local(): grad_rows = jnp.dot(grad_logit, piece, preferred_element_type=jnp.float32)  15.9 us
    dot_general x1, matrix products, local(): lax.dot_general(grad_logit, block_rows, (((0,), (0,)), ((), ())), preferr...  14.4 us
    reduce_scatter x1, waiting for transfers between devices, local(): lax.psum_scatter(grad_cols.astype(jnp.bfloat16), 'blk', scatter_dimension...  13.2 us
    psum x1, blocking collectives, local(): row_lse = jnp.log(lax.psum(row_sum, 'grp'))  12.4 us
  transfers between devices with their start and end apart: 4, of which 3 were waited for; matrix products, arithmetic and copies ran while one was open for 11% of the time, Pallas kernels for 0%

commit v1 on v0

v1 whole, which is shorter than its diff:
```python
import jax
import jax.numpy as jnp
from jax import lax
from jax.experimental import pallas as pl
from jax.experimental.pallas import tpu as pltpu
from jax.sharding import PartitionSpec as P

f32, bf16 = jnp.float32, jnp.bfloat16
MESH = pl.DeviceIdType.MESH
CAP = 30.0
ROWS, D, BATCH = 128, 1280, 16384
ARRIVAL = ((0, 0), (1, 0), (3, 0), (0, 1), (2, 0), (1, 1), (3, 1), (2, 1))
REDUCE = ((2, 1), (1, 1), (3, 1), (0, 1), (2, 0), (1, 0), (3, 0), (0, 0))
LAND_AT = (0, 32, 64, 128, 192, 256, 320, 384, 448, 480, 512, 544, 576, 640, 704, 768, 832)
LAND_ROWS = (32, 32, 64, 64, 64, 64, 64, 64, 32, 32, 32, 32, 64, 64, 64, 64, 64)
LAND = 896


def flip(bit, by):
    return bit + by - 2 * bit * by


def turn(place, by):
    return lax.rem(place + by, 4)


class Messages:
    def __init__(self, send, recv):
        self.send, self.recv, self.count, self.sent = send, recv, 0, []

    def take(self, count):
        first = self.count
        self.count += count
        return first

    def start(self, k, src, dst, device):
        copy = pltpu.make_async_remote_copy(
            src, dst, self.send.at[k], self.recv.at[k], device_id=device, device_id_type=MESH
        )
        copy.start()
        self.sent.append(copy)

    def arrived(self, k, region, device):
        pltpu.make_async_remote_copy(
            region, region, self.send.at[k], self.recv.at[k], device_id=device, device_id_type=MESH
        ).wait_recv()

    def finish(self):
        for copy in self.sent:
            copy.wait_send()


class Gather:
    def __init__(self, msgs, region, plus, minus, pair, me):
        self.m, self.region, self.me = msgs, region, me
        self.plus, self.minus, self.pair = plus, minus, pair
        self.k = msgs.take(15)

    TABLE = (
        ("plus", (0, 0, 0, 64), (3, 0, 0, 64)),
        ("plus", (0, 0, 64, 64), (3, 0, 64, 64)),
        ("plus", (3, 0, 0, 64), (2, 0, 0, 64)),
        ("plus", (0, 1, 0, 64), (3, 1, 0, 64)),
        ("plus", (3, 1, 0, 32), (2, 1, 0, 32)),
        ("minus", (0, 0, 64, 64), (1, 0, 64, 64)),
        ("minus", (0, 0, 0, 64), (1, 0, 0, 64)),
        ("minus", (1, 0, 64, 64), (2, 0, 64, 64)),
        ("minus", (0, 1, 0, 64), (1, 1, 0, 64)),
        ("minus", (1, 1, 32, 32), (2, 1, 32, 32)),
        ("pair", (0, 0, 0, 64), (0, 1, 0, 64)),
        ("pair", (0, 0, 64, 64), (0, 1, 64, 64)),
        ("pair", (1, 0, 64, 64), (1, 1, 64, 64)),
        ("pair", (3, 0, 64, 64), (3, 1, 64, 64)),
        ("pair", (2, 0, 64, 64), (2, 1, 64, 64)),
    )

    def go(self, *ks):
        for k in ks:
            way, here, _ = self.TABLE[k]
            ref = self.region(*here)
            self.m.start(self.k + k, ref, ref, getattr(self, way))

    def got(self, *ks):
        for k in ks:
            self.m.arrived(self.k + k, self.region(*self.TABLE[k][2]), self.me)


class Reduce:
    TABLE = (
        ("plus", (2, 1), 0, 32),
        ("minus", (2, 1), 32, 32),
        ("pair", (2, 1), 64, 64),
        ("pair", (1, 1), 64, 64),
        ("plus", (1, 1), 0, 64),
        ("pair", (3, 1), 64, 64),
        ("minus", (3, 1), 0, 64),
        ("pair", (0, 1), 64, 64),
        ("plus", (2, 0), 0, 32),
        ("minus", (2, 0), 32, 32),
        ("plus", (2, 0), 64, 32),
        ("minus", (2, 0), 96, 32),
        ("pair", (0, 1), 0, 64),
        ("plus", (1, 0), 0, 64),
        ("plus", (1, 0), 64, 64),
        ("minus", (3, 0), 0, 64),
        ("minus", (3, 0), 64, 64),
    )

    def __init__(self, msgs, part, land, plus, minus, pair, me):
        self.m, self.part, self.land, self.me = msgs, part, land, me
        self.plus, self.minus, self.pair = plus, minus, pair
        self.k = msgs.take(17)

    def where(self, k):
        return self.land.at[pl.ds(LAND_AT[k], LAND_ROWS[k])]

    def go(self, *ks):
        for k in ks:
            way, place, low, rows = self.TABLE[k]
            self.m.start(self.k + k, self.part(place, low, rows), self.where(k), getattr(self, way))

    def got(self, *ks):
        for k in ks:
            self.m.arrived(self.k + k, self.where(k), self.me)

    def add(self, place, low, rows, *landed):
        ref = self.part(place, low, rows)
        total = ref[...].astype(f32)
        for at in landed:
            total = total + self.land[pl.ds(at, rows)].astype(f32)
        ref[...] = total.astype(bf16)

    def step(self, place):
        if place == (2, 1):
            self.go(0, 1, 2)
        if place == (1, 1):
            self.go(3)
            self.got(0)
            self.add(place, 0, 32, LAND_AT[0])
            self.go(4)
        if place == (3, 1):
            self.go(5)
            self.got(1)
            self.add(place, 32, 32, LAND_AT[1])
            self.go(6)
        if place == (0, 1):
            self.go(7)
        if place == (2, 0):
            self.go(8, 9)
            self.got(2)
            self.add(place, 64, 64, LAND_AT[2])
            self.go(10, 11)
            self.got(4, 6)
            self.add((0, 1), 0, 64, LAND_AT[4], LAND_AT[6])
            self.go(12)
        if place == (1, 0):
            self.got(8)
            self.add(place, 0, 32, LAND_AT[8])
            self.go(13)
            self.got(3)
            self.add(place, 64, 64, LAND_AT[3])
            self.got(10)
            self.add(place, 64, 32, LAND_AT[10])
            self.go(14)
        if place == (3, 0):
            self.got(9)
            self.add(place, 32, 32, LAND_AT[9])
            self.go(15)
            self.got(5)
            self.add(place, 64, 64, LAND_AT[5])
            self.got(11)
            self.add(place, 96, 32, LAND_AT[11])
            self.go(16)

    def total(self):
        self.got(13, 15, 12, 7, 14, 16)
        halves = []
        for low, landed in ((0, (13, 15, 12)), (64, (14, 16, 7))):
            total = self.part((0, 0), low, 64)[...].astype(f32)
            for k in landed:
                total = total + self.where(k)[...].astype(f32)
            halves.append(total)
        return jnp.concatenate(halves, axis=0)


def kernel(
    ls_ref, pairing_ref, img_in, txt_in,
    gi_out, gt_out, loss_out, gls_out,
    img, txt, cosr, hr, gr, rowacc, colacc, arow, bmat, slacc, posacc,
    rows_all, cols_all, sc_all, sc_mid,
    gi, gi_sib, gt, land_i, land_t,
    send, recv,
):
    blk, grp = lax.axis_index("blk"), lax.axis_index("grp")
    x, c, y, z = grp // 2, lax.rem(grp, 2), blk // 4, lax.rem(blk, 4)
    yb = lax.rem(y, 2)
    tb = 1 - yb
    yp = y + 1 - 2 * yb
    yq = lax.rem(y + 3 + 2 * yb, 4)

    def device(x_, y_, z_, c_):
        return (y_ * 4 + z_, x_ * 2 + c_)

    me = device(x, y, z, c)
    sibling = device(x, y, z, 1 - c)
    img_peers = [
        (dx, dy, dc) for dy in range(2) for dx in range(4) for dc in range(2) if (dx, dy, dc) != (0, 0, 0)
    ]
    txt_peers = [(dz, dy) for dy in range(2) for dz in range(4) if (dz, dy) != (0, 0)]

    def img_peer(dx, dy, dc):
        return device(turn(x, dx), yp if dy else y, z, 1 - c if dc else c)

    def txt_peer(dz, dy):
        return device(x, yq if dy else y, turn(z, dz), c)

    barrier = pltpu.get_barrier_semaphore()
    for p in img_peers:
        pl.semaphore_signal(barrier, inc=1, device_id=img_peer(*p), device_id_type=MESH)
    for p in txt_peers:
        pl.semaphore_signal(barrier, inc=1, device_id=txt_peer(*p), device_id_type=MESH)

    def pair_of(dx, dy):
        return flip(yb, dy) * 4 + turn(x, dx)

    def slot_of(dz, dy):
        return flip(tb, dy) * 4 + turn(z, dz)

    def img_region(dx, dy, low, rows, other=False):
        half = 1 - c if other else c
        return img.at[pair_of(dx, dy), pl.ds(pl.multiple_of(half * ROWS + low, 32), rows)]

    def txt_region(dz, dy, low, rows):
        return txt.at[slot_of(dz, dy), pl.ds(low, rows)]

    def normalize(ref):
        wide = ref[...].astype(f32)
        inverse = lax.rsqrt(jnp.sum(wide * wide, axis=1, keepdims=True) + 1e-06)
        return inverse, wide * inverse

    img_region(0, 0, 0, ROWS)[...] = normalize(img_in)[1].astype(bf16)
    txt_region(0, 0, 0, ROWS)[...] = normalize(txt_in)[1].astype(bf16)

    msgs = Messages(send, recv)
    gat_i = Gather(msgs, img_region, img_peer(1, 0, 0), img_peer(3, 0, 0), img_peer(0, 1, 0), me)
    gat_t = Gather(msgs, txt_region, txt_peer(1, 0), txt_peer(3, 0), txt_peer(0, 1), me)
    both = (gat_i, gat_t)
    sib_k = msgs.take(8)

    def share(*places):
        for place in places:
            ref = img_region(*place, 0, ROWS)
            msgs.start(sib_k + ARRIVAL.index(place), ref, ref, sibling)

    def shared(*places):
        for place in places:
            msgs.arrived(sib_k + ARRIVAL.index(place), img_region(*place, 0, ROWS, other=True), me)

    pl.semaphore_wait(barrier, len(img_peers) + len(txt_peers))
    for g in both:
        g.go(10, 0, 5, 11, 1, 6)
    share((0, 0))

    ls = ls_ref[0]
    scale = jnp.exp(jnp.full((1, 256), ls, f32))
    factor = scale * (1.0 / CAP)
    rowacc[...] = jnp.zeros_like(rowacc)
    colacc[...] = jnp.zeros_like(colacc)
    slacc[...] = jnp.zeros_like(slacc)
    posacc[...] = jnp.zeros_like(posacc)

    def rows_of(slot):
        return pl.ds(pl.multiple_of(slot * ROWS, ROWS), ROWS)

    def forward(p, slots):
        t = txt[slots[0]] if len(slots) == 1 else jnp.concatenate([txt[s] for s in slots], axis=0)
        cos = lax.dot_general(t, img[p], (((1,), (1,)), ((), ())), preferred_element_type=f32)
        bent = jnp.tanh(cos * factor)
        power = jnp.exp(CAP * bent)
        held = power * (1.0 - bent * bent)
        for i, s in enumerate(slots):
            here = slice(i * ROWS, (i + 1) * ROWS)
            cosr[p, rows_of(s)] = cos[here]
            hr[p, rows_of(s)] = held[here]
            colacc[s] += power[here, :ROWS] + power[here, ROWS:]
        rowacc[p] += jnp.sum(power.reshape(len(slots) * 16, 8, 256), axis=0)

    def pair_at(i):
        dx = jnp.where((i == 1) | (i == 5), 1, 0) + jnp.where((i == 2) | (i == 6), 3, 0)
        dx = dx + jnp.where((i == 4) | (i == 7), 2, 0)
        dy = jnp.where((i == 3) | (i >= 5), 1, 0)
        return flip(yb, dy) * 4 + turn(x, dx)

    slots = [slot_of(*place) for place in ARRIVAL]

    def batch(first, last, members, unroll=1):
        def body(i, carry):
            forward(pair_at(i), [slots[j] for j in members])
            return carry

        lax.fori_loop(first, last, body, 0, unroll=unroll)

    for g in both:
        g.got(0)
        g.go(2)
        g.got(5)
        g.go(7, 12)
        g.got(10)
        g.go(3, 8)
    for g in both:
        g.got(1)
        g.go(13)
        g.got(6, 11)
    share((1, 0), (3, 0), (0, 1))
    shared((0, 0), (1, 0), (3, 0), (0, 1))
    batch(0, 4, (0, 1, 2, 3))
    for g in both:
        g.got(7)
        g.go(14)
        g.got(2)
    share((2, 0))
    for g in both:
        g.got(3)
        g.go(4)
        g.got(8)
        g.go(9)
    shared((2, 0))
    batch(4, 5, (0, 1, 2, 3))
    gat_i.got(12, 13)
    share((1, 1), (3, 1))
    gat_t.got(12, 13)
    shared((1, 1), (3, 1))
    batch(5, 7, (0, 1, 2, 3))
    batch(0, 7, (4, 5, 6))
    gat_i.got(4, 9, 14)
    share((2, 1))
    gat_t.got(4, 9, 14)
    batch(0, 7, (7,), unroll=7)
    shared((2, 1))
    batch(7, 8, (0, 1, 2, 3))
    batch(7, 8, (4, 5, 6, 7))

    img_me = yb * 8 + x * 2 + c
    txt_me = tb * 4 + z

    def img_index(dx, dy, dc):
        return flip(yb, dy) * 8 + turn(x, dx) * 2 + flip(c, dc)

    rows_all[img_me] = jnp.concatenate([jnp.sum(rowacc[p], axis=0, keepdims=True) for p in range(8)], axis=0)
    k_rows = msgs.take(len(img_peers))
    for i, p in enumerate(img_peers):
        msgs.start(k_rows + i, rows_all.at[img_me], rows_all.at[img_me], img_peer(*p))
    cols_all[txt_me] = jnp.concatenate(
        [jnp.sum(colacc[s].T, axis=0, keepdims=True) for s in range(8)], axis=0
    )
    k_cols = msgs.take(len(txt_peers))
    for i, p in enumerate(txt_peers):
        msgs.start(k_cols + i, cols_all.at[txt_me], cols_all.at[txt_me], txt_peer(*p))

    def collect_img(first, ref):
        for i, (dx, dy, dc) in enumerate(img_peers):
            msgs.arrived(first + i, ref.at[img_index((4 - dx) % 4, dy, dc)], me)

    def collect_txt(first, ref):
        for i, (dz, dy) in enumerate(txt_peers):
            msgs.arrived(first + i, ref.at[slot_of((4 - dz) % 4, dy)], me)

    def add_up(ref, first, last):
        total = ref[first]
        for i in range(first + 1, last):
            total = total + ref[i]
        return total

    collect_txt(k_cols, cols_all)
    col_sum = add_up(cols_all, 0, 8)
    col_weight = (0.5 * scale[:, :ROWS]) / col_sum
    for s in range(8):
        bmat[s] = jnp.broadcast_to(col_weight[s : s + 1], (ROWS, ROWS)).T
    collect_img(k_rows, rows_all)
    row_sum = add_up(rows_all, 0, 16)
    row_weight = (0.5 * scale) / row_sum
    for p in range(8):
        arow[p] = row_weight[p : p + 1]

    lane = lax.broadcasted_iota(jnp.int32, (ROWS, 256), 1)
    diagonal = lane == lax.broadcasted_iota(jnp.int32, (ROWS, 256), 0) + c * ROWS
    pair_mine = (pair_of(0, 0), pair_of(0, 1))

    def grad_tile(p, s, partner_of=None):
        b = bmat[s]
        cos = cosr[p, rows_of(s)]
        g = hr[p, rows_of(s)] * (arow[p] + jnp.concatenate([b, b], axis=1))
        if partner_of is not None:
            slot_blk = jnp.where(s // 4 == tb, y, yq) * 4 + lax.rem(s, 4)
            match = jnp.where(partner_of == slot_blk, 1.0, 0.0).astype(f32)
            partner = jnp.where(diagonal, match, 0.0)
            bent = jnp.tanh(cos * factor)
            g = g - scale * (partner * (1.0 - bent * bent))
            posacc[...] += jnp.sum((CAP * bent * partner).reshape(16, 8, 256), axis=0)
        slacc[...] += jnp.sum((g * cos).reshape(16, 8, 256), axis=0)
        gr[p, rows_of(s)] = g.astype(bf16)

    for dy in range(2):
        partner_of = pairing_ref[(yp if dy else y) * 4 + z]

        def special(s, carry):
            grad_tile(pair_mine[dy], s, partner_of)
            return carry

        lax.fori_loop(0, 8, special, 0)

    def plain(i, carry):
        p = flip(yb, i // 24) * 4 + turn(x, 1 + lax.rem(i // 8, 3))
        grad_tile(p, lax.rem(i, 8))
        return carry

    lax.fori_loop(0, 48, plain, 0, unroll=2)

    sub = lax.broadcasted_iota(jnp.int32, (8, 256), 0)
    half = lax.broadcasted_iota(jnp.int32, (8, 256), 1) // ROWS
    row_part = jnp.where((sub == pair_mine[0]) & (half == c), jnp.log(row_sum), 0.0) - 2.0 * posacc[...]
    col_part = jnp.where(sub[:, :ROWS] == txt_me, jnp.log(col_sum), 0.0)
    slope = slacc[...]
    sc_all[img_me, pl.ds(0, 8)] = row_part[:, :ROWS] + row_part[:, ROWS:] + col_part
    sc_all[img_me, pl.ds(8, 8)] = slope[:, :ROWS] + slope[:, ROWS:]
    k_sc = msgs.take(len(img_peers))
    for i, p in enumerate(img_peers):
        msgs.start(k_sc + i, sc_all.at[img_me], sc_all.at[img_me], img_peer(*p))

    k_sib = msgs.take(8)
    own = pl.ds(pl.multiple_of(c * ROWS, ROWS), ROWS)
    others = pl.ds(pl.multiple_of((1 - c) * ROWS, ROWS), ROWS)

    def img_part(place, low, rows):
        return gi.at[REDUCE.index(place), pl.ds(pl.multiple_of(c * ROWS + low, 32), rows)]

    def txt_part(place, low, rows):
        return gt.at[REDUCE.index(place), pl.ds(low, rows)]

    red_i = Reduce(msgs, img_part, land_i, img_peer(1, 0, 0), img_peer(3, 0, 0), img_peer(0, 1, 0), me)
    red_t = Reduce(msgs, txt_part, land_t, txt_peer(1, 0), txt_peer(3, 0), txt_peer(0, 1), me)
    k_mid = msgs.take(len(txt_peers))

    for i, place in enumerate(REDUCE):
        p, s = pair_of(*place), slot_of(*place)
        gi[i] = lax.dot_general(
            gr[p], txt[...].reshape(8 * ROWS, D), (((0,), (0,)), ((), ())), preferred_element_type=f32
        ).astype(bf16)
        msgs.start(k_sib + i, gi.at[i, others], gi_sib.at[i], sibling)
        lhs = jnp.concatenate([gr[q, rows_of(s)] for q in range(8)], axis=1)
        gt[i] = lax.dot_general(
            lhs, img[...].reshape(16 * ROWS, D), (((1,), (0,)), ((), ())), preferred_element_type=f32
        ).astype(bf16)
        msgs.arrived(k_sib + i, gi_sib.at[i], me)
        gi[i, own] = (gi[i, own].astype(f32) + gi_sib[i].astype(f32)).astype(bf16)
        red_i.step(place)
        red_t.step(place)
        if i == 3:
            collect_img(k_sc, sc_all)
            sc_mid[txt_me] = add_up(sc_all, 0, 16)
            for j, peer in enumerate(txt_peers):
                msgs.start(k_mid + j, sc_mid.at[txt_me], sc_mid.at[txt_me], txt_peer(*peer))

    collect_txt(k_mid, sc_mid)
    totals = add_up(sc_mid, 0, 4) + add_up(sc_mid, 4, 8)
    loss_out[0] = jnp.sum(totals[:8]) * (1.0 / (2.0 * BATCH))
    gls_out[0] = jnp.sum(totals[8:]) * (1.0 / BATCH)

    def back_norm(ref, grad_unit):
        inverse, unit = normalize(ref)
        inner = jnp.sum(unit * grad_unit, axis=1, keepdims=True)
        return inverse * (grad_unit - unit * inner)

    gi_out[...] = back_norm(img_in, red_i.total())
    gt_out[...] = back_norm(txt_in, red_t.total())
    msgs.finish()


N_MSG = 15 + 15 + 8 + 15 + 7 + 15 + 8 + 17 + 17 + 7


def local(image_embed, text_embed, log_scale, pairing):
    vmem, smem = pltpu.VMEM, pltpu.SMEM
    return pl.pallas_call(
        kernel,
        out_shape=[
            jax.ShapeDtypeStruct((ROWS, D), f32),
            jax.ShapeDtypeStruct((ROWS, D), f32),
            jax.ShapeDtypeStruct((1,), f32),
            jax.ShapeDtypeStruct((1,), f32),
        ],
        in_specs=[pl.BlockSpec(memory_space=smem)] * 2 + [pl.BlockSpec(memory_space=vmem)] * 2,
        out_specs=[pl.BlockSpec(memory_space=vmem)] * 2 + [pl.BlockSpec(memory_space=smem)] * 2,
        scratch_shapes=[
            vmem((8, 256, D), bf16),
            vmem((8, ROWS, D), bf16),
            vmem((8, 1024, 256), f32),
            vmem((8, 1024, 256), f32),
            vmem((8, 1024, 256), bf16),
            vmem((8, 8, 256), f32),
            vmem((8, ROWS, ROWS), f32),
            vmem((8, 1, 256), f32),
            vmem((8, ROWS, ROWS), f32),
            vmem((8, 256), f32),
            vmem((8, 256), f32),
            vmem((16, 8, 256), f32),
            vmem((8, 8, ROWS), f32),
            vmem((16, 16, ROWS), f32),
            vmem((8, 16, ROWS), f32),
            vmem((8, 256, D), bf16),
            vmem((8, ROWS, D), bf16),
            vmem((8, ROWS, D), bf16),
            vmem((LAND, D), bf16),
            vmem((LAND, D), bf16),
            pltpu.SemaphoreType.DMA((N_MSG,)),
            pltpu.SemaphoreType.DMA((N_MSG,)),
        ],
        compiler_params=pltpu.CompilerParams(
            collective_id=0, has_side_effects=True, vmem_limit_bytes=60 * 1024 * 1024
        ),
    )(log_scale, pairing, image_embed, text_embed)


def solution(mesh):
    return jax.shard_map(
        local,
        mesh=mesh,
        in_specs=(P(("blk", "grp"), None), P(("blk", "grp"), None), P(), P()),
        out_specs=(P(("blk", "grp"), None), P(("blk", "grp"), None), P(), P()),
        check_vma=False,
    )
```

time: 302 us -> 90.4 us (0.30)
  blocking collectives: 116 us -> 0 us
  waiting for transfers between devices: 96.9 us -> 0 us
  Pallas kernels: 0 us -> 81.7 us
  matrix products: 42.2 us -> 0 us
  other arithmetic: 23.9 us -> 0 us
  between operations: 20.7 us -> 4.8 us
    psum x3 -> x0, blocking collectives: 116 us -> none  [the longest x1 71.9 us: local(): totals = lax.psum((loss_part, slope), ('blk', 'grp'))]
    all_gather x2 -> x0, waiting for transfers between devices: 83.6 us -> none  [the longest x1 59.4 us: local(): piece = lax.all_gather(txt_norm, 'blk', axis=0, tiled=True)]
    pallas_call x0 -> x1, Pallas kernels: none -> 81.7 us  [local(): pl.pallas_call(kernel, out_shape=[jax.ShapeDtypeStruct((ROWS, D), f32), j...]
    dot_general x3 -> x0, matrix products: 42.2 us -> none  [the longest x1 15.9 us: local(): grad_rows = jnp.dot(grad_logit, piece, preferred_element_type=jnp.float32)]
    reduce_sum x7 -> x0, other arithmetic: 16 us -> none  [the longest x1 9.97 us: local(): jnp.sum(slope_term * cosine)]
    reduce_scatter x2 -> x0, waiting for transfers between devices: 13.2 us -> none  [the longest x1 13.2 us: local(): lax.psum_scatter(grad_cols.astype(jnp.bfloat16), 'blk', scatter_dimension...]
    mul x2 -> x0, other arithmetic: 4.18 us -> none  [back_norm(): return inverse * (grad_unit - unit * inner)]
    convert_element_type x2 -> x0, other arithmetic: 3.65 us -> none  [normalize(): return (inverse, unit, unit.astype(jnp.bfloat16))]
  transfers between devices with their start and end apart: 4 -> 0, of which waited for: 3 -> 0; matrix products, arithmetic and copies ran while one was open for 11% -> 0% of each run, Pallas kernels for 0% -> 0%
where the time goes in v1:
time: 90.4 us; the launch traced here: 89.3 us
  Pallas kernels  81.7 us (90%)
  between operations  4.8 us (5%)
  local copies, waits for them, and re-layouts  2.87 us (3%)
    pallas_call x1, Pallas kernels, local(): pl.pallas_call(kernel, out_shape=[jax.ShapeDtypeStruct((ROWS, D), f32), j...  81.7 us
    unnamed x4, local copies, waits for them, and re-layouts  2.87 us

profile of v1, /device:TPU:1, one launch (start us, length us, event | category | flops | bytes accessed | tf_op | source)
XLA Modules:
  0.0 89.3 jit_solution(3761006597075720415)
XLA Ops:
  1.3 81.7 %shard_map.75 = (f32[128,1280]{1,0:T(8,128)}, f32[128,1280]{1,0:T(8,128)}, f32[1]{0:T(128)}, f32[1]{0:T(128)}) custom-call(f32[1]{0:T(128)S(6)} %copy.12.ls_ref, s32[16]{0:T(128)} %pairing_ref.1, bf16[128,1280]{1,0:T(8,128)(2,1)} %img_in.1, bf16[128,1280]{1,0:T(8,128)(2,1)} %txt_in.1), custom_call_target="tpu_custom_call" | custom-call | tf_op jit(solution)/shard_map/pallas_call | solution.py:484
  82.9 0.0 copy-start
  82.9 2.0 %copy.13 = f32[128,1280]{1,0:T(8,128)} copy(f32[128,1280]{1,0:T(8,128)} %get-tuple-element.8) | data formatting | bytes 1310720
  85.0 0.0 copy-done
  85.0 0.8 copy.14
Async XLA Ops:
  82.9 2.0 %copy-start = (f32[128,1280]{1,0:T(8,128)S(1)}, f32[128,1280]{1,0:T(8,128)}, u32[]{:S(2)}) copy-start(f32[128,1280]{1,0:T(8,128)} %get-tuple-element.9) | copy-start | bytes 1966084

commit v2 on v1

--- a/solution.py
+++ b/solution.py
@@ -10,7 +10,7 @@
 CAP = 30.0
 ROWS, D, BATCH = 128, 1280, 16384
 ARRIVAL = ((0, 0), (1, 0), (3, 0), (0, 1), (2, 0), (1, 1), (3, 1), (2, 1))
-REDUCE = ((2, 1), (1, 1), (3, 1), (0, 1), (2, 0), (1, 0), (3, 0), (0, 0))
+REDUCE = ((2, 1), (2, 0), (1, 1), (3, 1), (1, 0), (3, 0), (0, 1), (0, 0))
 LAND_AT = (0, 32, 64, 128, 192, 256, 320, 384, 448, 480, 512, 544, 576, 640, 704, 768, 832)
 LAND_ROWS = (32, 32, 64, 64, 64, 64, 64, 64, 32, 32, 32, 32, 64, 64, 64, 64, 64)
 LAND = 896
@@ -26,7 +26,7 @@
 
 class Messages:
     def __init__(self, send, recv):
-        self.send, self.recv, self.count, self.sent = send, recv, 0, []
+        self.send, self.recv, self.count, self.open = send, recv, 0, {}
 
     def take(self, count):
         first = self.count
@@ -38,16 +38,19 @@
             src, dst, self.send.at[k], self.recv.at[k], device_id=device, device_id_type=MESH
         )
         copy.start()
-        self.sent.append(copy)
+        self.open[k] = copy
 
     def arrived(self, k, region, device):
         pltpu.make_async_remote_copy(
             region, region, self.send.at[k], self.recv.at[k], device_id=device, device_id_type=MESH
         ).wait_recv()
 
+    def sent(self, *ks):
+        for k in ks:
+            self.open.pop(k).wait_send()
+
     def finish(self):
-        for copy in self.sent:
-            copy.wait_send()
+        self.sent(*list(self.open))
 
 
 class Gather:
@@ -79,6 +82,9 @@
             way, here, _ = self.TABLE[k]
             ref = self.region(*here)
             self.m.start(self.k + k, ref, ref, getattr(self, way))
+
+    def sent(self, *ks):
+        self.m.sent(*(self.k + k for k in ks))
 
     def got(self, *ks):
         for k in ks:
@@ -119,6 +125,9 @@
             way, place, low, rows = self.TABLE[k]
             self.m.start(self.k + k, self.part(place, low, rows), self.where(k), getattr(self, way))
 
+    def sent(self, *ks):
+        self.m.sent(*(self.k + k for k in ks))
+
     def got(self, *ks):
         for k in ks:
             self.m.arrived(self.k + k, self.where(k), self.me)
@@ -130,47 +139,54 @@
             total = total + self.land[pl.ds(at, rows)].astype(f32)
         ref[...] = total.astype(bf16)
 
-    def step(self, place):
-        if place == (2, 1):
+    def step(self, i):
+        if i == 0:
             self.go(0, 1, 2)
-        if place == (1, 1):
+        if i == 1:
+            self.go(8, 9)
+        if i == 3:
+            self.got(0)
+            self.add((1, 1), 0, 32, LAND_AT[0])
+            self.go(4)
+            self.got(1)
+            self.add((3, 1), 32, 32, LAND_AT[1])
+            self.go(6)
+            self.sent(2)
             self.go(3)
-            self.got(0)
-            self.add(place, 0, 32, LAND_AT[0])
-            self.go(4)
-        if place == (3, 1):
+        if i == 4:
+            self.got(2)
+            self.add((2, 0), 64, 64, LAND_AT[2])
+            self.go(10, 11)
+        if i == 5:
+            self.got(8)
+            self.add((1, 0), 0, 32, LAND_AT[8])
+            self.go(13)
+            self.got(9)
+            self.add((3, 0), 32, 32, LAND_AT[9])
+            self.go(15)
+        if i == 6:
+            self.sent(3)
             self.go(5)
-            self.got(1)
-            self.add(place, 32, 32, LAND_AT[1])
-            self.go(6)
-        if place == (0, 1):
-            self.go(7)
-        if place == (2, 0):
-            self.go(8, 9)
-            self.got(2)
-            self.add(place, 64, 64, LAND_AT[2])
-            self.go(10, 11)
-            self.got(4, 6)
-            self.add((0, 1), 0, 64, LAND_AT[4], LAND_AT[6])
-            self.go(12)
-        if place == (1, 0):
-            self.got(8)
-            self.add(place, 0, 32, LAND_AT[8])
-            self.go(13)
-            self.got(3)
-            self.add(place, 64, 64, LAND_AT[3])
-            self.got(10)
-            self.add(place, 64, 32, LAND_AT[10])
-            self.go(14)
-        if place == (3, 0):
-            self.got(9)
-            self.add(place, 32, 32, LAND_AT[9])
-            self.go(15)
-            self.got(5)
-            self.add(place, 64, 64, LAND_AT[5])
-            self.got(11)
-            self.add(place, 96, 32, LAND_AT[11])
-            self.go(16)
+
+    def last(self):
+        self.got(3)
+        self.add((1, 0), 64, 64, LAND_AT[3])
+        self.got(10)
+        self.add((1, 0), 64, 32, LAND_AT[10])
+        self.go(14)
+
+    def last_pair(self):
+        self.got(4, 6)
+        self.add((0, 1), 0, 64, LAND_AT[4], LAND_AT[6])
+        self.sent(5)
+        self.go(7, 12)
+
+    def last_ring(self):
+        self.got(5)
+        self.add((3, 0), 64, 64, LAND_AT[5])
+        self.got(11)
+        self.add((3, 0), 96, 32, LAND_AT[11])
+        self.go(16)
 
     def total(self):
         self.got(13, 15, 12, 7, 14, 16)
@@ -183,10 +199,16 @@
         return jnp.concatenate(halves, axis=0)
 
 
+def normalize(ref):
+    wide = ref[...].astype(f32)
+    inverse = lax.rsqrt(jnp.sum(wide * wide, axis=1, keepdims=True) + 1e-06)
+    return inverse, wide * inverse
+
+
 def kernel(
-    ls_ref, pairing_ref, img_in, txt_in,
-    gi_out, gt_out, loss_out, gls_out,
-    img, txt, cosr, hr, gr, rowacc, colacc, arow, bmat, slacc, posacc,
+    pairing_ref, ls_ref, img_in, txt_in,
+    gi_out, gt_out, sums_out,
+    img, img_t, txt, cosr, hr, gr, rowacc, colacc, rowk, colk, arow, bmat, diag, slacc, posacc,
     rows_all, cols_all, sc_all, sc_mid,
     gi, gi_sib, gt, land_i, land_t,
     send, recv,
@@ -233,11 +255,6 @@
     def txt_region(dz, dy, low, rows):
         return txt.at[slot_of(dz, dy), pl.ds(low, rows)]
 
-    def normalize(ref):
-        wide = ref[...].astype(f32)
-        inverse = lax.rsqrt(jnp.sum(wide * wide, axis=1, keepdims=True) + 1e-06)
-        return inverse, wide * inverse
-
     img_region(0, 0, 0, ROWS)[...] = normalize(img_in)[1].astype(bf16)
     txt_region(0, 0, 0, ROWS)[...] = normalize(txt_in)[1].astype(bf16)
 
@@ -258,32 +275,29 @@
 
     pl.semaphore_wait(barrier, len(img_peers) + len(txt_peers))
     for g in both:
-        g.go(10, 0, 5, 11, 1, 6)
+        g.go(10, 0, 5)
     share((0, 0))
 
-    ls = ls_ref[0]
-    scale = jnp.exp(jnp.full((1, 256), ls, f32))
+    scale = jnp.exp(jnp.full((1, 256), ls_ref[0], f32))
     factor = scale * (1.0 / CAP)
-    rowacc[...] = jnp.zeros_like(rowacc)
-    colacc[...] = jnp.zeros_like(colacc)
-    slacc[...] = jnp.zeros_like(slacc)
-    posacc[...] = jnp.zeros_like(posacc)
+    for ref in (rowacc, colacc, rowk, colk, slacc, posacc):
+        ref[...] = jnp.zeros_like(ref)
 
     def rows_of(slot):
         return pl.ds(pl.multiple_of(slot * ROWS, ROWS), ROWS)
 
-    def forward(p, slots):
-        t = txt[slots[0]] if len(slots) == 1 else jnp.concatenate([txt[s] for s in slots], axis=0)
-        cos = lax.dot_general(t, img[p], (((1,), (1,)), ((), ())), preferred_element_type=f32)
+    def forward(p, s):
+        cos = lax.dot_general(txt[s], img_t[p], (((1,), (0,)), ((), ())), preferred_element_type=f32)
         bent = jnp.tanh(cos * factor)
         power = jnp.exp(CAP * bent)
         held = power * (1.0 - bent * bent)
-        for i, s in enumerate(slots):
-            here = slice(i * ROWS, (i + 1) * ROWS)
-            cosr[p, rows_of(s)] = cos[here]
-            hr[p, rows_of(s)] = held[here]
-            colacc[s] += power[here, :ROWS] + power[here, ROWS:]
-        rowacc[p] += jnp.sum(power.reshape(len(slots) * 16, 8, 256), axis=0)
+        slope = held * cos
+        cosr[p, rows_of(s)] = cos
+        hr[p, rows_of(s)] = held
+        colacc[s] += power[:, :ROWS] + power[:, ROWS:]
+        colk[s] += slope[:, :ROWS] + slope[:, ROWS:]
+        rowacc[p] += jnp.sum(power.reshape(16, 8, 256), axis=0)
+        rowk[p] += jnp.sum(slope.reshape(16, 8, 256), axis=0)
 
     def pair_at(i):
         dx = jnp.where((i == 1) | (i == 5), 1, 0) + jnp.where((i == 2) | (i == 6), 3, 0)
@@ -295,50 +309,63 @@
 
     def batch(first, last, members, unroll=1):
         def body(i, carry):
-            forward(pair_at(i), [slots[j] for j in members])
+            for j in members:
+                forward(pair_at(i), slots[j])
             return carry
 
         lax.fori_loop(first, last, body, 0, unroll=unroll)
 
-    for g in both:
-        g.got(0)
-        g.go(2)
-        g.got(5)
-        g.go(7, 12)
-        g.got(10)
-        g.go(3, 8)
-    for g in both:
-        g.got(1)
-        g.go(13)
-        g.got(6, 11)
+    def turned(*places):
+        shared(*places)
+        for place in places:
+            p = pair_of(*place)
+            img_t[p] = img[p].T
+
+    turned((0, 0))
+    for g in both:
+        g.sent(10, 0, 5)
+        g.go(11, 1, 6)
+    batch(0, 1, (0,))
+    for g in both:
+        g.got(10, 0, 5)
+    for g in both:
+        g.sent(11, 1, 6)
+        g.go(12, 2, 7)
+    for g in both:
+        g.got(11, 1, 6)
     share((1, 0), (3, 0), (0, 1))
-    shared((0, 0), (1, 0), (3, 0), (0, 1))
-    batch(0, 4, (0, 1, 2, 3))
+    turned((1, 0), (3, 0), (0, 1))
+    batch(0, 1, (1, 2, 3))
+    batch(1, 2, (0, 1, 2, 3))
+    for g in both:
+        g.sent(12, 2, 7)
+        g.go(13, 3, 8)
+    batch(2, 4, (0, 1, 2, 3))
     for g in both:
         g.got(7)
         g.go(14)
         g.got(2)
     share((2, 0))
+    turned((2, 0))
+    batch(0, 4, (4,), unroll=4)
+    batch(4, 5, (0, 1, 2, 3, 4))
     for g in both:
         g.got(3)
         g.go(4)
         g.got(8)
         g.go(9)
-    shared((2, 0))
-    batch(4, 5, (0, 1, 2, 3))
-    gat_i.got(12, 13)
+    for g in both:
+        g.got(12, 13)
     share((1, 1), (3, 1))
-    gat_t.got(12, 13)
-    shared((1, 1), (3, 1))
-    batch(5, 7, (0, 1, 2, 3))
-    batch(0, 7, (4, 5, 6))
+    batch(0, 5, (5, 6))
+    turned((1, 1), (3, 1))
+    batch(5, 7, (0, 1, 2, 3, 4, 5, 6))
     gat_i.got(4, 9, 14)
     share((2, 1))
     gat_t.got(4, 9, 14)
     batch(0, 7, (7,), unroll=7)
-    shared((2, 1))
-    batch(7, 8, (0, 1, 2, 3))
-    batch(7, 8, (4, 5, 6, 7))
+    turned((2, 1))
+    batch(7, 8, (0, 1, 2, 3, 4, 5, 6, 7))
 
     img_me = yb * 8 + x * 2 + c
     txt_me = tb * 4 + z
@@ -371,6 +398,31 @@
             total = total + ref[i]
         return total
 
+    lane = lax.broadcasted_iota(jnp.int32, (ROWS, 256), 1)
+    diagonal = lane == lax.broadcasted_iota(jnp.int32, (ROWS, 256), 0) + c * ROWS
+    pair_mine = (pair_of(0, 0), pair_of(0, 1))
+
+    def matching(s, carry):
+        slot_blk = jnp.where(s // 4 == tb, y, yq) * 4 + lax.rem(s, 4)
+        for dy in range(2):
+            partner_of = pairing_ref[(yp if dy else y) * 4 + z]
+            match = jnp.where(partner_of == slot_blk, 1.0, 0.0).astype(f32)
+            partner = jnp.where(diagonal, match, 0.0)
+            cos = cosr[pair_mine[dy], rows_of(s)]
+            bent = jnp.tanh(cos * factor)
+            taken = scale * (partner * (1.0 - bent * bent))
+            diag[dy, rows_of(s)] = taken
+            posacc[...] += jnp.sum((CAP * bent * partner).reshape(16, 8, 256), axis=0)
+            slacc[...] += jnp.sum((taken * cos).reshape(16, 8, 256), axis=0)
+        return carry
+
+    lax.fori_loop(0, 8, matching, 0, unroll=2)
+    row_slope = jnp.concatenate([jnp.sum(rowk[p], axis=0, keepdims=True) for p in range(8)], axis=0)
+    col_slope = jnp.concatenate([jnp.sum(colk[s].T, axis=0, keepdims=True) for s in range(8)], axis=0)
+    for g in both:
+        g.sent(13, 3, 8, 14, 4, 9)
+    msgs.sent(*range(sib_k, sib_k + 8))
+
     collect_txt(k_cols, cols_all)
     col_sum = add_up(cols_all, 0, 8)
     col_weight = (0.5 * scale[:, :ROWS]) / col_sum
@@ -382,50 +434,31 @@
     for p in range(8):
         arow[p] = row_weight[p : p + 1]
 
-    lane = lax.broadcasted_iota(jnp.int32, (ROWS, 256), 1)
-    diagonal = lane == lax.broadcasted_iota(jnp.int32, (ROWS, 256), 0) + c * ROWS
-    pair_mine = (pair_of(0, 0), pair_of(0, 1))
-
-    def grad_tile(p, s, partner_of=None):
-        b = bmat[s]
-        cos = cosr[p, rows_of(s)]
-        g = hr[p, rows_of(s)] * (arow[p] + jnp.concatenate([b, b], axis=1))
-        if partner_of is not None:
-            slot_blk = jnp.where(s // 4 == tb, y, yq) * 4 + lax.rem(s, 4)
-            match = jnp.where(partner_of == slot_blk, 1.0, 0.0).astype(f32)
-            partner = jnp.where(diagonal, match, 0.0)
-            bent = jnp.tanh(cos * factor)
-            g = g - scale * (partner * (1.0 - bent * bent))
-            posacc[...] += jnp.sum((CAP * bent * partner).reshape(16, 8, 256), axis=0)
-        slacc[...] += jnp.sum((g * cos).reshape(16, 8, 256), axis=0)
-        gr[p, rows_of(s)] = g.astype(bf16)
-
-    for dy in range(2):
-        partner_of = pairing_ref[(yp if dy else y) * 4 + z]
-
-        def special(s, carry):
-            grad_tile(pair_mine[dy], s, partner_of)
+    def gradient(place):
+        p = pair_of(*place)
+
+        def body(s, carry):
+            b = bmat[s]
+            g = hr[p, rows_of(s)] * (arow[p] + jnp.concatenate([b, b], axis=1))
+            if place[0] == 0:
+                g = g - diag[place[1], rows_of(s)]
+            gr[p, rows_of(s)] = g.astype(bf16)
             return carry
 
-        lax.fori_loop(0, 8, special, 0)
-
-    def plain(i, carry):
-        p = flip(yb, i // 24) * 4 + turn(x, 1 + lax.rem(i // 8, 3))
-        grad_tile(p, lax.rem(i, 8))
-        return carry
-
-    lax.fori_loop(0, 48, plain, 0, unroll=2)
-
-    sub = lax.broadcasted_iota(jnp.int32, (8, 256), 0)
-    half = lax.broadcasted_iota(jnp.int32, (8, 256), 1) // ROWS
-    row_part = jnp.where((sub == pair_mine[0]) & (half == c), jnp.log(row_sum), 0.0) - 2.0 * posacc[...]
-    col_part = jnp.where(sub[:, :ROWS] == txt_me, jnp.log(col_sum), 0.0)
-    slope = slacc[...]
-    sc_all[img_me, pl.ds(0, 8)] = row_part[:, :ROWS] + row_part[:, ROWS:] + col_part
-    sc_all[img_me, pl.ds(8, 8)] = slope[:, :ROWS] + slope[:, ROWS:]
+        lax.fori_loop(0, 8, body, 0, unroll=4)
+
+    def send_sums():
+        sub = lax.broadcasted_iota(jnp.int32, (8, 256), 0)
+        half = lax.broadcasted_iota(jnp.int32, (8, 256), 1) // ROWS
+        row_part = jnp.where((sub == pair_mine[0]) & (half == c), jnp.log(row_sum), 0.0) - 2.0 * posacc[...]
+        col_part = jnp.where(sub[:, :ROWS] == txt_me, jnp.log(col_sum), 0.0)
+        slope = row_weight * row_slope - slacc[...]
+        sc_all[img_me, pl.ds(0, 8)] = row_part[:, :ROWS] + row_part[:, ROWS:] + col_part
+        sc_all[img_me, pl.ds(8, 8)] = slope[:, :ROWS] + slope[:, ROWS:] + col_weight * col_slope
+        for i, p in enumerate(img_peers):
+            msgs.start(k_sc + i, sc_all.at[img_me], sc_all.at[img_me], img_peer(*p))
+
     k_sc = msgs.take(len(img_peers))
-    for i, p in enumerate(img_peers):
-        msgs.start(k_sc + i, sc_all.at[img_me], sc_all.at[img_me], img_peer(*p))
 
     k_sib = msgs.take(8)
     own = pl.ds(pl.multiple_of(c * ROWS, ROWS), ROWS)
@@ -443,37 +476,57 @@
 
     for i, place in enumerate(REDUCE):
         p, s = pair_of(*place), slot_of(*place)
+        if i == 0:
+            gradient(place)
         gi[i] = lax.dot_general(
             gr[p], txt[...].reshape(8 * ROWS, D), (((0,), (0,)), ((), ())), preferred_element_type=f32
         ).astype(bf16)
         msgs.start(k_sib + i, gi.at[i, others], gi_sib.at[i], sibling)
+        if i == 0:
+            for other in REDUCE[1:]:
+                gradient(other)
         lhs = jnp.concatenate([gr[q, rows_of(s)] for q in range(8)], axis=1)
         gt[i] = lax.dot_general(
             lhs, img[...].reshape(16 * ROWS, D), (((1,), (0,)), ((), ())), preferred_element_type=f32
         ).astype(bf16)
         msgs.arrived(k_sib + i, gi_sib.at[i], me)
         gi[i, own] = (gi[i, own].astype(f32) + gi_sib[i].astype(f32)).astype(bf16)
-        red_i.step(place)
-        red_t.step(place)
+        red_i.step(i)
+        red_t.step(i)
+        if i == 0:
+            send_sums()
         if i == 3:
             collect_img(k_sc, sc_all)
             sc_mid[txt_me] = add_up(sc_all, 0, 16)
             for j, peer in enumerate(txt_peers):
                 msgs.start(k_mid + j, sc_mid.at[txt_me], sc_mid.at[txt_me], txt_peer(*peer))
 
+    for r in (red_i, red_t):
+        r.last()
+    for r in (red_i, red_t):
+        r.last_pair()
+    for r in (red_i, red_t):
+        r.last_ring()
     collect_txt(k_mid, sc_mid)
-    totals = add_up(sc_mid, 0, 4) + add_up(sc_mid, 4, 8)
-    loss_out[0] = jnp.sum(totals[:8]) * (1.0 / (2.0 * BATCH))
-    gls_out[0] = jnp.sum(totals[8:]) * (1.0 / BATCH)
-
-    def back_norm(ref, grad_unit):
+    sums_out[...] = add_up(sc_mid, 0, 4) + add_up(sc_mid, 4, 8)
+    for first, count in ((k_rows, 15), (k_cols, 7), (k_sc, 15), (k_mid, 7), (k_sib, 8)):
+        msgs.sent(*range(first, first + count))
+    gi_out[...] = red_i.total()
+    gt_out[...] = red_t.total()
+    msgs.finish()
+
+
+def epilogue(sums, img_in, txt_in, gi_in, gt_in, gi_out, gt_out, loss_out, gls_out):
+    def back_norm(ref, grad):
         inverse, unit = normalize(ref)
+        grad_unit = grad[...]
         inner = jnp.sum(unit * grad_unit, axis=1, keepdims=True)
         return inverse * (grad_unit - unit * inner)
 
-    gi_out[...] = back_norm(img_in, red_i.total())
-    gt_out[...] = back_norm(txt_in, red_t.total())
-    msgs.finish()
+    gi_out[...] = back_norm(img_in, gi_in)
+    gt_out[...] = back_norm(txt_in, gt_in)
+    loss_out[0] = jnp.sum(sums[:8]) * (1.0 / (2.0 * BATCH))
+    gls_out[0] = jnp.sum(sums[8:]) * (1.0 / BATCH)
 
 
 N_MSG = 15 + 15 + 8 + 15 + 7 + 15 + 8 + 17 + 17 + 7
@@ -481,26 +534,28 @@
 
 def local(image_embed, text_embed, log_scale, pairing):
     vmem, smem = pltpu.VMEM, pltpu.SMEM
-    return pl.pallas_call(
+    in_vmem, in_smem = pl.BlockSpec(memory_space=vmem), pl.BlockSpec(memory_space=smem)
+    grad = jax.ShapeDtypeStruct((ROWS, D), f32)
+    scalar = jax.ShapeDtypeStruct((1,), f32)
+    unit_img, unit_txt, sums = pl.pallas_call(
         kernel,
-        out_shape=[
-            jax.ShapeDtypeStruct((ROWS, D), f32),
-            jax.ShapeDtypeStruct((ROWS, D), f32),
-            jax.ShapeDtypeStruct((1,), f32),
-            jax.ShapeDtypeStruct((1,), f32),
-        ],
-        in_specs=[pl.BlockSpec(memory_space=smem)] * 2 + [pl.BlockSpec(memory_space=vmem)] * 2,
-        out_specs=[pl.BlockSpec(memory_space=vmem)] * 2 + [pl.BlockSpec(memory_space=smem)] * 2,
+        out_shape=[grad, grad, jax.ShapeDtypeStruct((16, ROWS), f32)],
+        in_specs=[in_smem] * 2 + [in_vmem] * 2,
+        out_specs=[in_vmem] * 3,
         scratch_shapes=[
             vmem((8, 256, D), bf16),
+            vmem((8, D, 256), bf16),
             vmem((8, ROWS, D), bf16),
             vmem((8, 1024, 256), f32),
             vmem((8, 1024, 256), f32),
             vmem((8, 1024, 256), bf16),
             vmem((8, 8, 256), f32),
             vmem((8, ROWS, ROWS), f32),
+            vmem((8, 8, 256), f32),
+            vmem((8, ROWS, ROWS), f32),
             vmem((8, 1, 256), f32),
             vmem((8, ROWS, ROWS), f32),
+            vmem((2, 1024, 256), f32),
             vmem((8, 256), f32),
             vmem((8, 256), f32),
             vmem((16, 8, 256), f32),
@@ -518,7 +573,16 @@
         compiler_params=pltpu.CompilerParams(
             collective_id=0, has_side_effects=True, vmem_limit_bytes=60 * 1024 * 1024
         ),
-    )(log_scale, pairing, image_embed, text_embed)
+        name="contrast",
+    )(pairing, log_scale, image_embed, text_embed)
+    return pl.pallas_call(
+        epilogue,
+        out_shape=[grad, grad, scalar, scalar],
+        in_specs=[in_vmem] * 5,
+        out_specs=[in_vmem] * 2 + [in_smem] * 2,
+        compiler_params=pltpu.CompilerParams(vmem_limit_bytes=60 * 1024 * 1024),
+        name="back_norm",
+    )(sums, image_embed, text_embed, unit_img, unit_txt)
 
 
 def solution(mesh):

time: 90.4 us -> 80.6 us (0.89)
  between operations: 4.8 us -> 1.45 us
  local copies, waits for them, and re-layouts: 2.87 us -> 0 us
  Pallas kernels: 81.7 us -> 78.9 us
    unnamed x4 -> x0, local copies, waits for them, and re-layouts: 2.87 us -> none
    pallas_call x1 -> x2, Pallas kernels: 81.7 us -> 78.9 us  [the longest x1 76 us: local(): pl.pallas_call(kernel, out_shape=[grad, grad, jax.ShapeDtypeStruct((16, R...]
where the time goes in v2:
time: 80.6 us; the launch traced here: 80.4 us
  Pallas kernels  78.9 us (98%)
  between operations  1.45 us (2%)
    pallas_call x1, Pallas kernels, local(): pl.pallas_call(kernel, out_shape=[grad, grad, jax.ShapeDtypeStruct((16, R...  76 us
    pallas_call x1, Pallas kernels, local(): pl.pallas_call(epilogue, out_shape=[grad, grad, scalar, scalar], in_specs...  2.93 us

profile of v2, /device:TPU:1, one launch (start us, length us, event | category | flops | bytes accessed | tf_op | source)
XLA Modules:
  0.0 80.4 jit_solution(15898358540120323595)
XLA Ops:
  1.3 76.0 %contrast.1 = (f32[128,1280]{1,0:T(8,128)}, f32[128,1280]{1,0:T(8,128)}, f32[16,128]{1,0:T(8,128)}) custom-call(s32[16]{0:T(128)} %pairing_ref.1, f32[1]{0:T(128)S(6)} %copy.8.ls_ref, bf16[128,1280]{1,0:T(8,128)(2,1)} %img_in.3, bf16[128,1280]{1,0:T(8,128)(2,1)} %txt_in.3), custom_call_target="tpu_custom_call" | custom-call | tf_op jit(solution)/shard_map/contrast/pallas_call | solution.py:540
  77.3 2.9 %back_norm.1 = (f32[128,1280]{1,0:T(8,128)}, f32[128,1280]{1,0:T(8,128)}, f32[1]{0:T(128)}, f32[1]{0:T(128)}) custom-call(f32[16,128]{1,0:T(8,128)} %get-tuple-element.7.sums, bf16[128,1280]{1,0:T(8,128)(2,1)} %img_in.3, bf16[128,1280]{1,0:T(8,128)(2,1)} %txt_in.3, f32[128,1280]{1,0:T(8,128)} %get-tuple-element.8.gi_in, f32[128,1280]{1,0:T(8,128)} %get-tuple-element.9.gt_in), custom_call_target="tpu_custom_call" | custom-call | tf_op jit(solution)/shard_map/back_norm/pallas_call | solution.py:578

commit v3 on v2

--- a/solution.py
+++ b/solution.py
@@ -57,24 +57,26 @@
     def __init__(self, msgs, region, plus, minus, pair, me):
         self.m, self.region, self.me = msgs, region, me
         self.plus, self.minus, self.pair = plus, minus, pair
-        self.k = msgs.take(15)
+        self.k = msgs.take(17)
 
     TABLE = (
         ("plus", (0, 0, 0, 64), (3, 0, 0, 64)),
         ("plus", (0, 0, 64, 64), (3, 0, 64, 64)),
         ("plus", (3, 0, 0, 64), (2, 0, 0, 64)),
-        ("plus", (0, 1, 0, 64), (3, 1, 0, 64)),
+        ("plus", (0, 1, 0, 32), (3, 1, 0, 32)),
         ("plus", (3, 1, 0, 32), (2, 1, 0, 32)),
         ("minus", (0, 0, 64, 64), (1, 0, 64, 64)),
         ("minus", (0, 0, 0, 64), (1, 0, 0, 64)),
         ("minus", (1, 0, 64, 64), (2, 0, 64, 64)),
-        ("minus", (0, 1, 0, 64), (1, 1, 0, 64)),
+        ("minus", (0, 1, 32, 32), (1, 1, 32, 32)),
         ("minus", (1, 1, 32, 32), (2, 1, 32, 32)),
         ("pair", (0, 0, 0, 64), (0, 1, 0, 64)),
         ("pair", (0, 0, 64, 64), (0, 1, 64, 64)),
         ("pair", (1, 0, 64, 64), (1, 1, 64, 64)),
         ("pair", (3, 0, 64, 64), (3, 1, 64, 64)),
         ("pair", (2, 0, 64, 64), (2, 1, 64, 64)),
+        ("plus", (0, 1, 32, 32), (3, 1, 32, 32)),
+        ("minus", (0, 1, 0, 32), (1, 1, 0, 32)),
     )
 
     def go(self, *ks):
@@ -144,42 +146,39 @@
             self.go(0, 1, 2)
         if i == 1:
             self.go(8, 9)
-        if i == 3:
+        if i == 2:
+            self.go(3)
             self.got(0)
             self.add((1, 1), 0, 32, LAND_AT[0])
             self.go(4)
+        if i == 3:
+            self.go(5)
             self.got(1)
             self.add((3, 1), 32, 32, LAND_AT[1])
             self.go(6)
-            self.sent(2)
-            self.go(3)
         if i == 4:
             self.got(2)
             self.add((2, 0), 64, 64, LAND_AT[2])
             self.go(10, 11)
-        if i == 5:
             self.got(8)
             self.add((1, 0), 0, 32, LAND_AT[8])
             self.go(13)
+        if i == 5:
             self.got(9)
             self.add((3, 0), 32, 32, LAND_AT[9])
             self.go(15)
         if i == 6:
-            self.sent(3)
-            self.go(5)
+            self.go(7)
 
     def last(self):
+        self.got(4, 6)
+        self.add((0, 1), 0, 64, LAND_AT[4], LAND_AT[6])
+        self.go(12)
         self.got(3)
         self.add((1, 0), 64, 64, LAND_AT[3])
         self.got(10)
         self.add((1, 0), 64, 32, LAND_AT[10])
         self.go(14)
-
-    def last_pair(self):
-        self.got(4, 6)
-        self.add((0, 1), 0, 64, LAND_AT[4], LAND_AT[6])
-        self.sent(5)
-        self.go(7, 12)
 
     def last_ring(self):
         self.got(5)
@@ -262,20 +261,29 @@
     gat_i = Gather(msgs, img_region, img_peer(1, 0, 0), img_peer(3, 0, 0), img_peer(0, 1, 0), me)
     gat_t = Gather(msgs, txt_region, txt_peer(1, 0), txt_peer(3, 0), txt_peer(0, 1), me)
     both = (gat_i, gat_t)
-    sib_k = msgs.take(8)
-
-    def share(*places):
+    sib_k = msgs.take(9)
+
+    def pieces(places):
         for place in places:
-            ref = img_region(*place, 0, ROWS)
-            msgs.start(sib_k + ARRIVAL.index(place), ref, ref, sibling)
+            if place == (2, 1):
+                yield sib_k + 7, (*place, 0, 64)
+                yield sib_k + 8, (*place, 64, 64)
+            else:
+                yield sib_k + ARRIVAL.index(place), (*place, 0, ROWS)
+
+    def share(*places, only=(0, 1)):
+        for i, (k, piece) in enumerate(pieces(places)):
+            if i in only or len(places) > 1:
+                ref = img_region(*piece)
+                msgs.start(k, ref, ref, sibling)
 
     def shared(*places):
-        for place in places:
-            msgs.arrived(sib_k + ARRIVAL.index(place), img_region(*place, 0, ROWS, other=True), me)
+        for k, piece in pieces(places):
+            msgs.arrived(k, img_region(*piece, other=True), me)
 
     pl.semaphore_wait(barrier, len(img_peers) + len(txt_peers))
     for g in both:
-        g.go(10, 0, 5)
+        g.go(10, 0, 5, 11, 1, 6)
     share((0, 0))
 
     scale = jnp.exp(jnp.full((1, 256), ls_ref[0], f32))
@@ -322,46 +330,42 @@
             img_t[p] = img[p].T
 
     turned((0, 0))
-    for g in both:
-        g.sent(10, 0, 5)
-        g.go(11, 1, 6)
     batch(0, 1, (0,))
     for g in both:
-        g.got(10, 0, 5)
+        g.got(0, 5, 10)
+        g.go(2, 7, 12, 3, 8, 15, 16)
     for g in both:
-        g.sent(11, 1, 6)
-        g.go(12, 2, 7)
-    for g in both:
-        g.got(11, 1, 6)
+        g.got(1)
+        g.go(13)
+        g.got(6, 11)
     share((1, 0), (3, 0), (0, 1))
+    batch(0, 1, (1, 2, 3))
     turned((1, 0), (3, 0), (0, 1))
-    batch(0, 1, (1, 2, 3))
-    batch(1, 2, (0, 1, 2, 3))
-    for g in both:
-        g.sent(12, 2, 7)
-        g.go(13, 3, 8)
-    batch(2, 4, (0, 1, 2, 3))
+    batch(1, 4, (0, 1, 2, 3))
     for g in both:
         g.got(7)
         g.go(14)
         g.got(2)
     share((2, 0))
-    turned((2, 0))
     batch(0, 4, (4,), unroll=4)
-    batch(4, 5, (0, 1, 2, 3, 4))
     for g in both:
         g.got(3)
         g.go(4)
         g.got(8)
         g.go(9)
-    for g in both:
-        g.got(12, 13)
+    turned((2, 0))
+    batch(4, 5, (0, 1, 2, 3, 4))
+    gat_i.got(12, 13, 15, 16)
     share((1, 1), (3, 1))
+    gat_t.got(12, 13, 15, 16)
     batch(0, 5, (5, 6))
     turned((1, 1), (3, 1))
-    batch(5, 7, (0, 1, 2, 3, 4, 5, 6))
-    gat_i.got(4, 9, 14)
-    share((2, 1))
+    batch(5, 6, (0, 1, 2, 3, 4, 5, 6))
+    gat_i.got(4, 9)
+    share((2, 1), only=(0,))
+    batch(6, 7, (0, 1, 2, 3, 4, 5, 6))
+    gat_i.got(14)
+    share((2, 1), only=(1,))
     gat_t.got(4, 9, 14)
     batch(0, 7, (7,), unroll=7)
     turned((2, 1))
@@ -420,8 +424,8 @@
     row_slope = jnp.concatenate([jnp.sum(rowk[p], axis=0, keepdims=True) for p in range(8)], axis=0)
     col_slope = jnp.concatenate([jnp.sum(colk[s].T, axis=0, keepdims=True) for s in range(8)], axis=0)
     for g in both:
-        g.sent(13, 3, 8, 14, 4, 9)
-    msgs.sent(*range(sib_k, sib_k + 8))
+        g.sent(*range(17))
+    msgs.sent(*range(sib_k, sib_k + 9))
 
     collect_txt(k_cols, cols_all)
     col_sum = add_up(cols_all, 0, 8)
@@ -474,37 +478,45 @@
     red_t = Reduce(msgs, txt_part, land_t, txt_peer(1, 0), txt_peer(3, 0), txt_peer(0, 1), me)
     k_mid = msgs.take(len(txt_peers))
 
-    for i, place in enumerate(REDUCE):
-        p, s = pair_of(*place), slot_of(*place)
-        if i == 0:
-            gradient(place)
+    def img_product(i):
         gi[i] = lax.dot_general(
-            gr[p], txt[...].reshape(8 * ROWS, D), (((0,), (0,)), ((), ())), preferred_element_type=f32
+            gr[pair_of(*REDUCE[i])], txt[...].reshape(8 * ROWS, D), (((0,), (0,)), ((), ())), preferred_element_type=f32
         ).astype(bf16)
         msgs.start(k_sib + i, gi.at[i, others], gi_sib.at[i], sibling)
-        if i == 0:
-            for other in REDUCE[1:]:
-                gradient(other)
+
+    def img_send(i):
+        msgs.arrived(k_sib + i, gi_sib.at[i], me)
+        gi[i, own] = (gi[i, own].astype(f32) + gi_sib[i].astype(f32)).astype(bf16)
+        red_i.step(i)
+
+    def txt_product(i):
+        s = slot_of(*REDUCE[i])
         lhs = jnp.concatenate([gr[q, rows_of(s)] for q in range(8)], axis=1)
         gt[i] = lax.dot_general(
             lhs, img[...].reshape(16 * ROWS, D), (((1,), (0,)), ((), ())), preferred_element_type=f32
         ).astype(bf16)
-        msgs.arrived(k_sib + i, gi_sib.at[i], me)
-        gi[i, own] = (gi[i, own].astype(f32) + gi_sib[i].astype(f32)).astype(bf16)
-        red_i.step(i)
         red_t.step(i)
-        if i == 0:
-            send_sums()
+
+    gradient(REDUCE[0])
+    img_product(0)
+    for place in REDUCE[1:]:
+        gradient(place)
+    img_send(0)
+    txt_product(0)
+    send_sums()
+    for i in range(1, 8):
+        img_product(i)
+        if i > 1:
+            img_send(i - 1)
+        txt_product(i)
         if i == 3:
             collect_img(k_sc, sc_all)
             sc_mid[txt_me] = add_up(sc_all, 0, 16)
             for j, peer in enumerate(txt_peers):
                 msgs.start(k_mid + j, sc_mid.at[txt_me], sc_mid.at[txt_me], txt_peer(*peer))
-
+    img_send(7)
     for r in (red_i, red_t):
         r.last()
-    for r in (red_i, red_t):
-        r.last_pair()
     for r in (red_i, red_t):
         r.last_ring()
     collect_txt(k_mid, sc_mid)
@@ -529,7 +541,7 @@
     gls_out[0] = jnp.sum(sums[8:]) * (1.0 / BATCH)
 
 
-N_MSG = 15 + 15 + 8 + 15 + 7 + 15 + 8 + 17 + 17 + 7
+N_MSG = 17 + 17 + 9 + 15 + 7 + 15 + 8 + 17 + 17 + 7
 
 
 def local(image_embed, text_embed, log_scale, pairing):

time: 80.6 us -> 73.9 us (0.917)
  Pallas kernels: 78.9 us -> 72.2 us
    pallas_call x1, Pallas kernels: 76 us -> 69.3 us  [local(): pl.pallas_call(kernel, out_shape=[grad, grad, jax.ShapeDtypeStruct((16, R...]
where the time goes in v3:
time: 73.9 us; the launch traced here: 73.7 us
  Pallas kernels  72.2 us (98%)
  between operations  1.45 us (2%)
    pallas_call x1, Pallas kernels, local(): pl.pallas_call(kernel, out_shape=[grad, grad, jax.ShapeDtypeStruct((16, R...  69.3 us
    pallas_call x1, Pallas kernels, local(): pl.pallas_call(epilogue, out_shape=[grad, grad, scalar, scalar], in_specs...  2.93 us

profile of v3, /device:TPU:1, one launch (start us, length us, event | category | flops | bytes accessed | tf_op | source)
XLA Modules:
  0.0 73.7 jit_solution(15781109953956282615)
XLA Ops:
  1.3 69.3 %contrast.1 = (f32[128,1280]{1,0:T(8,128)}, f32[128,1280]{1,0:T(8,128)}, f32[16,128]{1,0:T(8,128)}) custom-call(s32[16]{0:T(128)} %pairing_ref.1, f32[1]{0:T(128)S(6)} %copy.8.ls_ref, bf16[128,1280]{1,0:T(8,128)(2,1)} %img_in.3, bf16[128,1280]{1,0:T(8,128)(2,1)} %txt_in.3), custom_call_target="tpu_custom_call" | custom-call | tf_op jit(solution)/shard_map/contrast/pallas_call | solution.py:552
  70.6 2.9 %back_norm.1 = (f32[128,1280]{1,0:T(8,128)}, f32[128,1280]{1,0:T(8,128)}, f32[1]{0:T(128)}, f32[1]{0:T(128)}) custom-call(f32[16,128]{1,0:T(8,128)} %get-tuple-element.7.sums, bf16[128,1280]{1,0:T(8,128)(2,1)} %img_in.3, bf16[128,1280]{1,0:T(8,128)(2,1)} %txt_in.3, f32[128,1280]{1,0:T(8,128)} %get-tuple-element.8.gi_in, f32[128,1280]{1,0:T(8,128)} %get-tuple-element.9.gt_in), custom_call_target="tpu_custom_call" | custom-call | tf_op jit(solution)/shard_map/back_norm/pallas_call | solution.py:590

commit v4 on v3

--- a/solution.py
+++ b/solution.py
@@ -187,30 +187,27 @@
         self.add((3, 0), 96, 32, LAND_AT[11])
         self.go(16)
 
-    def total(self):
-        self.got(13, 15, 12, 7, 14, 16)
-        halves = []
-        for low, landed in ((0, (13, 15, 12)), (64, (14, 16, 7))):
-            total = self.part((0, 0), low, 64)[...].astype(f32)
-            for k in landed:
-                total = total + self.where(k)[...].astype(f32)
-            halves.append(total)
-        return jnp.concatenate(halves, axis=0)
-
-
-def normalize(ref):
-    wide = ref[...].astype(f32)
+    def total(self, low, *ks):
+        self.got(*ks)
+        total = self.part((0, 0), low, 64)[...].astype(f32)
+        for k in ks:
+            total = total + self.where(k)[...].astype(f32)
+        return total
+
+
+def normalize(embed):
+    wide = embed.astype(f32)
     inverse = lax.rsqrt(jnp.sum(wide * wide, axis=1, keepdims=True) + 1e-06)
     return inverse, wide * inverse
 
 
 def kernel(
-    pairing_ref, ls_ref, img_in, txt_in,
+    ls_ref, pairing_in, img_in, txt_in,
     gi_out, gt_out, sums_out,
     img, img_t, txt, cosr, hr, gr, rowacc, colacc, rowk, colk, arow, bmat, diag, slacc, posacc,
     rows_all, cols_all, sc_all, sc_mid,
     gi, gi_sib, gt, land_i, land_t,
-    send, recv,
+    pairing_ref, embeds, units, sums, own_sem, send, recv,
 ):
     blk, grp = lax.axis_index("blk"), lax.axis_index("grp")
     x, c, y, z = grp // 2, lax.rem(grp, 2), blk // 4, lax.rem(blk, 4)
@@ -235,6 +232,12 @@
     def txt_peer(dz, dy):
         return device(x, yq if dy else y, turn(z, dz), c)
 
+    own_copies = [
+        pltpu.make_async_copy(src, dst, own_sem.at[i])
+        for i, (src, dst) in enumerate(((img_in, embeds.at[0]), (txt_in, embeds.at[1]), (pairing_in, pairing_ref)))
+    ]
+    for copy in own_copies:
+        copy.start()
     barrier = pltpu.get_barrier_semaphore()
     for p in img_peers:
         pl.semaphore_signal(barrier, inc=1, device_id=img_peer(*p), device_id_type=MESH)
@@ -254,8 +257,10 @@
     def txt_region(dz, dy, low, rows):
         return txt.at[slot_of(dz, dy), pl.ds(low, rows)]
 
-    img_region(0, 0, 0, ROWS)[...] = normalize(img_in)[1].astype(bf16)
-    txt_region(0, 0, 0, ROWS)[...] = normalize(txt_in)[1].astype(bf16)
+    own_copies[0].wait()
+    img_region(0, 0, 0, ROWS)[...] = normalize(embeds[0])[1].astype(bf16)
+    own_copies[1].wait()
+    txt_region(0, 0, 0, ROWS)[...] = normalize(embeds[1])[1].astype(bf16)
 
     msgs = Messages(send, recv)
     gat_i = Gather(msgs, img_region, img_peer(1, 0, 0), img_peer(3, 0, 0), img_peer(0, 1, 0), me)
@@ -402,6 +407,7 @@
             total = total + ref[i]
         return total
 
+    own_copies[2].wait()
     lane = lax.broadcasted_iota(jnp.int32, (ROWS, 256), 1)
     diagonal = lane == lax.broadcasted_iota(jnp.int32, (ROWS, 256), 0) + c * ROWS
     pair_mine = (pair_of(0, 0), pair_of(0, 1))
@@ -438,18 +444,21 @@
     for p in range(8):
         arow[p] = row_weight[p : p + 1]
 
-    def gradient(place):
+    def tile(p, s, matched=None):
+        b = bmat[s]
+        g = hr[p, rows_of(s)] * (arow[p] + jnp.concatenate([b, b], axis=1))
+        if matched is not None:
+            g = g - diag[matched, rows_of(s)]
+        gr[p, rows_of(s)] = g.astype(bf16)
+
+    def gradient(place, first=1):
         p = pair_of(*place)
 
-        def body(s, carry):
-            b = bmat[s]
-            g = hr[p, rows_of(s)] * (arow[p] + jnp.concatenate([b, b], axis=1))
-            if place[0] == 0:
-                g = g - diag[place[1], rows_of(s)]
-            gr[p, rows_of(s)] = g.astype(bf16)
+        def body(i, carry):
+            tile(p, lax.rem(slot_of(2, 1) + i, 8), place[1] if place[0] == 0 else None)
             return carry
 
-        lax.fori_loop(0, 8, body, 0, unroll=4)
+        lax.fori_loop(first, 8, body, 0, unroll=4 if first == 0 else 7)
 
     def send_sums():
         sub = lax.broadcasted_iota(jnp.int32, (8, 256), 0)
@@ -497,12 +506,14 @@
         ).astype(bf16)
         red_t.step(i)
 
-    gradient(REDUCE[0])
+    gradient(REDUCE[0], 0)
+    for place in REDUCE[1:]:
+        tile(pair_of(*place), slot_of(2, 1), place[1] if place[0] == 0 else None)
     img_product(0)
+    txt_product(0)
     for place in REDUCE[1:]:
         gradient(place)
     img_send(0)
-    txt_product(0)
     send_sums()
     for i in range(1, 8):
         img_product(i)
@@ -520,25 +531,54 @@
     for r in (red_i, red_t):
         r.last_ring()
     collect_txt(k_mid, sc_mid)
-    sums_out[...] = add_up(sc_mid, 0, 4) + add_up(sc_mid, 4, 8)
+    sums[...] = add_up(sc_mid, 0, 4) + add_up(sc_mid, 4, 8)
+    out_copies = [pltpu.make_async_copy(sums, sums_out, own_sem.at[3])]
+    out_copies[0].start()
     for first, count in ((k_rows, 15), (k_cols, 7), (k_sc, 15), (k_mid, 7), (k_sib, 8)):
         msgs.sent(*range(first, first + count))
-    gi_out[...] = red_i.total()
-    gt_out[...] = red_t.total()
+    for r in (red_i, red_t):
+        r.sent(*range(12))
+    for low, ks in ((64, (7, 14, 16)), (0, (13, 15, 12))):
+        for n, (r, out) in enumerate(((red_i, gi_out), (red_t, gt_out))):
+            part = pl.ds(low, 64)
+            units[n, part] = r.total(low, *ks)
+            copy = pltpu.make_async_copy(units.at[n, part], out.at[part], own_sem.at[3 + len(out_copies)])
+            copy.start()
+            out_copies.append(copy)
     msgs.finish()
-
-
-def epilogue(sums, img_in, txt_in, gi_in, gt_in, gi_out, gt_out, loss_out, gls_out):
-    def back_norm(ref, grad):
-        inverse, unit = normalize(ref)
-        grad_unit = grad[...]
+    for copy in out_copies:
+        copy.wait()
+
+
+def epilogue(sums_in, img_in, txt_in, gi_in, gt_in, gi_out, gt_out, loss_out, gls_out, sums, embeds, units, sem):
+    sums_copy = pltpu.make_async_copy(sums_in, sums, sem.at[0])
+    ins, outs = [], []
+    for low in (0, 64):
+        for n, (embed, unit, out) in enumerate(((img_in, gi_in, gi_out), (txt_in, gt_in, gt_out))):
+            k = 1 + 3 * len(ins)
+            part = pl.ds(low, 64)
+            ins.append((
+                pltpu.make_async_copy(embed.at[part], embeds.at[n, part], sem.at[k]),
+                pltpu.make_async_copy(unit.at[part], units.at[n, part], sem.at[k + 1]),
+            ))
+            outs.append((n, part, pltpu.make_async_copy(units.at[n, part], out.at[part], sem.at[k + 2])))
+    for pair in ins:
+        for copy in pair:
+            copy.start()
+    sums_copy.start()
+    for pair, (n, part, out) in zip(ins, outs):
+        for copy in pair:
+            copy.wait()
+        inverse, unit = normalize(embeds[n, part])
+        grad_unit = units[n, part]
         inner = jnp.sum(unit * grad_unit, axis=1, keepdims=True)
-        return inverse * (grad_unit - unit * inner)
-
-    gi_out[...] = back_norm(img_in, gi_in)
-    gt_out[...] = back_norm(txt_in, gt_in)
+        units[n, part] = inverse * (grad_unit - unit * inner)
+        out.start()
+    sums_copy.wait()
     loss_out[0] = jnp.sum(sums[:8]) * (1.0 / (2.0 * BATCH))
     gls_out[0] = jnp.sum(sums[8:]) * (1.0 / BATCH)
+    for _, _, out in outs:
+        out.wait()
 
 
 N_MSG = 17 + 17 + 9 + 15 + 7 + 15 + 8 + 17 + 17 + 7
@@ -546,14 +586,14 @@
 
 def local(image_embed, text_embed, log_scale, pairing):
     vmem, smem = pltpu.VMEM, pltpu.SMEM
-    in_vmem, in_smem = pl.BlockSpec(memory_space=vmem), pl.BlockSpec(memory_space=smem)
+    anywhere, in_smem = pl.BlockSpec(memory_space=pl.ANY), pl.BlockSpec(memory_space=smem)
     grad = jax.ShapeDtypeStruct((ROWS, D), f32)
     scalar = jax.ShapeDtypeStruct((1,), f32)
     unit_img, unit_txt, sums = pl.pallas_call(
         kernel,
         out_shape=[grad, grad, jax.ShapeDtypeStruct((16, ROWS), f32)],
-        in_specs=[in_smem] * 2 + [in_vmem] * 2,
-        out_specs=[in_vmem] * 3,
+        in_specs=[in_smem] + [anywhere] * 3,
+        out_specs=[anywhere] * 3,
         scratch_shapes=[
             vmem((8, 256, D), bf16),
             vmem((8, D, 256), bf16),
@@ -579,6 +619,11 @@
             vmem((8, ROWS, D), bf16),
             vmem((LAND, D), bf16),
             vmem((LAND, D), bf16),
+            smem((16,), jnp.int32),
+            vmem((2, ROWS, D), bf16),
+            vmem((2, ROWS, D), f32),
+            vmem((16, ROWS), f32),
+            pltpu.SemaphoreType.DMA((8,)),
             pltpu.SemaphoreType.DMA((N_MSG,)),
             pltpu.SemaphoreType.DMA((N_MSG,)),
         ],
@@ -586,12 +631,18 @@
             collective_id=0, has_side_effects=True, vmem_limit_bytes=60 * 1024 * 1024
         ),
         name="contrast",
-    )(pairing, log_scale, image_embed, text_embed)
+    )(log_scale, pairing, image_embed, text_embed)
     return pl.pallas_call(
         epilogue,
         out_shape=[grad, grad, scalar, scalar],
-        in_specs=[in_vmem] * 5,
-        out_specs=[in_vmem] * 2 + [in_smem] * 2,
+        in_specs=[anywhere] * 5,
+        out_specs=[anywhere] * 2 + [in_smem] * 2,
+        scratch_shapes=[
+            vmem((16, ROWS), f32),
+            vmem((2, ROWS, D), bf16),
+            vmem((2, ROWS, D), f32),
+            pltpu.SemaphoreType.DMA((13,)),
+        ],
         compiler_params=pltpu.CompilerParams(vmem_limit_bytes=60 * 1024 * 1024),
         name="back_norm",
     )(sums, image_embed, text_embed, unit_img, unit_txt)

time: 73.9 us -> 72.8 us (0.985)
  Pallas kernels: 72.2 us -> 71.2 us
    pallas_call x1, Pallas kernels: 69.3 us -> 67.8 us  [local(): pl.pallas_call(kernel, out_shape=[grad, grad, jax.ShapeDtypeStruct((16, R...]
where the time goes in v4:
time: 72.8 us; the launch traced here: 72.6 us
  Pallas kernels  71.2 us (98%)
  between operations  1.47 us (2%)
    pallas_call x1, Pallas kernels, local(): pl.pallas_call(kernel, out_shape=[grad, grad, jax.ShapeDtypeStruct((16, R...  67.8 us
    pallas_call x1, Pallas kernels, local(): pl.pallas_call(epilogue, out_shape=[grad, grad, scalar, scalar], in_specs...  3.33 us

profile of v4, /device:TPU:1, one launch (start us, length us, event | category | flops | bytes accessed | tf_op | source)
XLA Modules:
  0.0 72.6 jit_solution(2393177700203502622)
XLA Ops:
  1.3 67.8 %contrast.1 = (f32[128,1280]{1,0:T(8,128)}, f32[128,1280]{1,0:T(8,128)}, f32[16,128]{1,0:T(8,128)}) custom-call(f32[1]{0:T(128)S(6)} %copy.8.ls_ref, s32[16]{0:T(128)} %pairing_in.1, bf16[128,1280]{1,0:T(8,128)(2,1)} %img_in.3, bf16[128,1280]{1,0:T(8,128)(2,1)} %txt_in.3), custom_call_target="tpu_custom_call" | custom-call | tf_op jit(solution)/shard_map/contrast/pallas_call | solution.py:592
  69.1 3.3 %back_norm.1 = (f32[128,1280]{1,0:T(8,128)}, f32[128,1280]{1,0:T(8,128)}, f32[1]{0:T(128)}, f32[1]{0:T(128)}) custom-call(f32[16,128]{1,0:T(8,128)} %get-tuple-element.7.sums_in, bf16[128,1280]{1,0:T(8,128)(2,1)} %img_in.3, bf16[128,1280]{1,0:T(8,128)(2,1)} %txt_in.3, f32[128,1280]{1,0:T(8,128)} %get-tuple-element.8.gi_in, f32[128,1280]{1,0:T(8,128)} %get-tuple-element.9.gt_in), custom_call_target="tpu_custom_call" | custom-call | tf_op jit(solution)/shard_map/back_norm/pallas_call | solution.py:635

commit v5 on v4

--- a/solution.py
+++ b/solution.py
@@ -10,7 +10,7 @@
 CAP = 30.0
 ROWS, D, BATCH = 128, 1280, 16384
 ARRIVAL = ((0, 0), (1, 0), (3, 0), (0, 1), (2, 0), (1, 1), (3, 1), (2, 1))
-REDUCE = ((2, 1), (2, 0), (1, 1), (3, 1), (1, 0), (3, 0), (0, 1), (0, 0))
+REDUCE = ((2, 1), (2, 0), (1, 1), (3, 1), (0, 1), (1, 0), (3, 0), (0, 0))
 LAND_AT = (0, 32, 64, 128, 192, 256, 320, 384, 448, 480, 512, 544, 576, 640, 704, 768, 832)
 LAND_ROWS = (32, 32, 64, 64, 64, 64, 64, 64, 32, 32, 32, 32, 64, 64, 64, 64, 64)
 LAND = 896
@@ -54,8 +54,8 @@
 
 
 class Gather:
-    def __init__(self, msgs, region, plus, minus, pair, me):
-        self.m, self.region, self.me = msgs, region, me
+    def __init__(self, msgs, region, plus, minus, pair, me, relay=None):
+        self.m, self.region, self.me, self.relay = msgs, region, me, relay
         self.plus, self.minus, self.pair = plus, minus, pair
         self.k = msgs.take(17)
 
@@ -91,6 +91,8 @@
     def got(self, *ks):
         for k in ks:
             self.m.arrived(self.k + k, self.region(*self.TABLE[k][2]), self.me)
+            if self.relay is not None:
+                self.relay(k, self.TABLE[k][2])
 
 
 class Reduce:
@@ -157,18 +159,18 @@
             self.add((3, 1), 32, 32, LAND_AT[1])
             self.go(6)
         if i == 4:
+            self.go(7)
             self.got(2)
             self.add((2, 0), 64, 64, LAND_AT[2])
             self.go(10, 11)
+        if i == 5:
             self.got(8)
             self.add((1, 0), 0, 32, LAND_AT[8])
             self.go(13)
-        if i == 5:
+        if i == 6:
             self.got(9)
             self.add((3, 0), 32, 32, LAND_AT[9])
             self.go(15)
-        if i == 6:
-            self.go(7)
 
     def last(self):
         self.got(4, 6)
@@ -263,33 +265,25 @@
     txt_region(0, 0, 0, ROWS)[...] = normalize(embeds[1])[1].astype(bf16)
 
     msgs = Messages(send, recv)
-    gat_i = Gather(msgs, img_region, img_peer(1, 0, 0), img_peer(3, 0, 0), img_peer(0, 1, 0), me)
+    sib_k = msgs.take(18)
+
+    def share(k, region):
+        ref = img_region(*region)
+        msgs.start(sib_k + k, ref, ref, sibling)
+
+    gat_i = Gather(msgs, img_region, img_peer(1, 0, 0), img_peer(3, 0, 0), img_peer(0, 1, 0), me, share)
     gat_t = Gather(msgs, txt_region, txt_peer(1, 0), txt_peer(3, 0), txt_peer(0, 1), me)
     both = (gat_i, gat_t)
-    sib_k = msgs.take(9)
-
-    def pieces(places):
-        for place in places:
-            if place == (2, 1):
-                yield sib_k + 7, (*place, 0, 64)
-                yield sib_k + 8, (*place, 64, 64)
-            else:
-                yield sib_k + ARRIVAL.index(place), (*place, 0, ROWS)
-
-    def share(*places, only=(0, 1)):
-        for i, (k, piece) in enumerate(pieces(places)):
-            if i in only or len(places) > 1:
-                ref = img_region(*piece)
-                msgs.start(k, ref, ref, sibling)
-
-    def shared(*places):
-        for k, piece in pieces(places):
-            msgs.arrived(k, img_region(*piece, other=True), me)
+
+    def shared(place):
+        pieces = [(k, entry[2]) for k, entry in enumerate(Gather.TABLE) if entry[2][:2] == place]
+        for k, region in pieces or [(17, (0, 0, 0, ROWS))]:
+            msgs.arrived(sib_k + k, img_region(*region, other=True), me)
 
     pl.semaphore_wait(barrier, len(img_peers) + len(txt_peers))
     for g in both:
         g.go(10, 0, 5, 11, 1, 6)
-    share((0, 0))
+    share(17, (0, 0, 0, ROWS))
 
     scale = jnp.exp(jnp.full((1, 256), ls_ref[0], f32))
     factor = scale * (1.0 / CAP)
@@ -328,11 +322,10 @@
 
         lax.fori_loop(first, last, body, 0, unroll=unroll)
 
-    def turned(*places):
-        shared(*places)
-        for place in places:
-            p = pair_of(*place)
-            img_t[p] = img[p].T
+    def turned(place):
+        shared(place)
+        p = pair_of(*place)
+        img_t[p] = img[p].T
 
     turned((0, 0))
     batch(0, 1, (0,))
@@ -343,34 +336,34 @@
         g.got(1)
         g.go(13)
         g.got(6, 11)
-    share((1, 0), (3, 0), (0, 1))
     batch(0, 1, (1, 2, 3))
-    turned((1, 0), (3, 0), (0, 1))
-    batch(1, 4, (0, 1, 2, 3))
+    turned((1, 0))
+    batch(1, 2, (0, 1, 2, 3))
+    turned((3, 0))
+    batch(2, 3, (0, 1, 2, 3))
     for g in both:
         g.got(7)
         g.go(14)
-        g.got(2)
-    share((2, 0))
+        g.got(2, 12)
+    turned((0, 1))
+    batch(3, 4, (0, 1, 2, 3))
     batch(0, 4, (4,), unroll=4)
+    turned((2, 0))
     for g in both:
         g.got(3)
         g.go(4)
         g.got(8)
         g.go(9)
-    turned((2, 0))
     batch(4, 5, (0, 1, 2, 3, 4))
-    gat_i.got(12, 13, 15, 16)
-    share((1, 1), (3, 1))
-    gat_t.got(12, 13, 15, 16)
-    batch(0, 5, (5, 6))
-    turned((1, 1), (3, 1))
+    for g in both:
+        g.got(13, 15, 16)
+    batch(0, 5, (5, 6), unroll=5)
+    turned((1, 1))
     batch(5, 6, (0, 1, 2, 3, 4, 5, 6))
     gat_i.got(4, 9)
-    share((2, 1), only=(0,))
+    turned((3, 1))
     batch(6, 7, (0, 1, 2, 3, 4, 5, 6))
     gat_i.got(14)
-    share((2, 1), only=(1,))
     gat_t.got(4, 9, 14)
     batch(0, 7, (7,), unroll=7)
     turned((2, 1))
@@ -431,7 +424,7 @@
     col_slope = jnp.concatenate([jnp.sum(colk[s].T, axis=0, keepdims=True) for s in range(8)], axis=0)
     for g in both:
         g.sent(*range(17))
-    msgs.sent(*range(sib_k, sib_k + 9))
+    msgs.sent(*range(sib_k, sib_k + 18))
 
     collect_txt(k_cols, cols_all)
     col_sum = add_up(cols_all, 0, 8)
@@ -514,13 +507,14 @@
     for place in REDUCE[1:]:
         gradient(place)
     img_send(0)
-    send_sums()
     for i in range(1, 8):
         img_product(i)
         if i > 1:
             img_send(i - 1)
         txt_product(i)
-        if i == 3:
+        if i == 1:
+            send_sums()
+        if i == 4:
             collect_img(k_sc, sc_all)
             sc_mid[txt_me] = add_up(sc_all, 0, 16)
             for j, peer in enumerate(txt_peers):
@@ -550,50 +544,29 @@
         copy.wait()
 
 
-def epilogue(sums_in, img_in, txt_in, gi_in, gt_in, gi_out, gt_out, loss_out, gls_out, sums, embeds, units, sem):
-    sums_copy = pltpu.make_async_copy(sums_in, sums, sem.at[0])
-    ins, outs = [], []
-    for low in (0, 64):
-        for n, (embed, unit, out) in enumerate(((img_in, gi_in, gi_out), (txt_in, gt_in, gt_out))):
-            k = 1 + 3 * len(ins)
-            part = pl.ds(low, 64)
-            ins.append((
-                pltpu.make_async_copy(embed.at[part], embeds.at[n, part], sem.at[k]),
-                pltpu.make_async_copy(unit.at[part], units.at[n, part], sem.at[k + 1]),
-            ))
-            outs.append((n, part, pltpu.make_async_copy(units.at[n, part], out.at[part], sem.at[k + 2])))
-    for pair in ins:
-        for copy in pair:
-            copy.start()
-    sums_copy.start()
-    for pair, (n, part, out) in zip(ins, outs):
-        for copy in pair:
-            copy.wait()
-        inverse, unit = normalize(embeds[n, part])
-        grad_unit = units[n, part]
+def epilogue(sums, img_in, txt_in, gi_in, gt_in, gi_out, gt_out, loss_out, gls_out):
+    for embed, grad, out in ((img_in, gi_in, gi_out), (txt_in, gt_in, gt_out)):
+        inverse, unit = normalize(embed[...])
+        grad_unit = grad[...]
         inner = jnp.sum(unit * grad_unit, axis=1, keepdims=True)
-        units[n, part] = inverse * (grad_unit - unit * inner)
-        out.start()
-    sums_copy.wait()
+        out[...] = inverse * (grad_unit - unit * inner)
     loss_out[0] = jnp.sum(sums[:8]) * (1.0 / (2.0 * BATCH))
     gls_out[0] = jnp.sum(sums[8:]) * (1.0 / BATCH)
-    for _, _, out in outs:
-        out.wait()
-
-
-N_MSG = 17 + 17 + 9 + 15 + 7 + 15 + 8 + 17 + 17 + 7
+
+
+N_MSG = 17 + 17 + 18 + 15 + 7 + 15 + 8 + 17 + 17 + 7
 
 
 def local(image_embed, text_embed, log_scale, pairing):
     vmem, smem = pltpu.VMEM, pltpu.SMEM
-    anywhere, in_smem = pl.BlockSpec(memory_space=pl.ANY), pl.BlockSpec(memory_space=smem)
+    in_hbm, in_vmem, in_smem = (pl.BlockSpec(memory_space=m) for m in (pltpu.HBM, vmem, smem))
     grad = jax.ShapeDtypeStruct((ROWS, D), f32)
     scalar = jax.ShapeDtypeStruct((1,), f32)
     unit_img, unit_txt, sums = pl.pallas_call(
         kernel,
         out_shape=[grad, grad, jax.ShapeDtypeStruct((16, ROWS), f32)],
-        in_specs=[in_smem] + [anywhere] * 3,
-        out_specs=[anywhere] * 3,
+        in_specs=[in_smem] + [in_hbm] * 3,
+        out_specs=[in_hbm] * 3,
         scratch_shapes=[
             vmem((8, 256, D), bf16),
             vmem((8, D, 256), bf16),
@@ -635,14 +608,8 @@
     return pl.pallas_call(
         epilogue,
         out_shape=[grad, grad, scalar, scalar],
-        in_specs=[anywhere] * 5,
-        out_specs=[anywhere] * 2 + [in_smem] * 2,
-        scratch_shapes=[
-            vmem((16, ROWS), f32),
-            vmem((2, ROWS, D), bf16),
-            vmem((2, ROWS, D), f32),
-            pltpu.SemaphoreType.DMA((13,)),
-        ],
+        in_specs=[in_vmem] * 5,
+        out_specs=[in_vmem] * 2 + [in_smem] * 2,
         compiler_params=pltpu.CompilerParams(vmem_limit_bytes=60 * 1024 * 1024),
         name="back_norm",
     )(sums, image_embed, text_embed, unit_img, unit_txt)

time: 72.8 us -> 70.7 us (0.971)
  Pallas kernels: 71.2 us -> 69 us
    pallas_call x1, Pallas kernels: 67.8 us -> 66.1 us  [local(): pl.pallas_call(kernel, out_shape=[grad, grad, jax.ShapeDtypeStruct((16, R...]
where the time goes in v5:
time: 70.7 us; the launch traced here: 70.5 us
  Pallas kernels  69 us (98%)
  between operations  1.47 us (2%)
    pallas_call x1, Pallas kernels, local(): pl.pallas_call(kernel, out_shape=[grad, grad, jax.ShapeDtypeStruct((16, R...  66.1 us
    pallas_call x1, Pallas kernels, local(): pl.pallas_call(epilogue, out_shape=[grad, grad, scalar, scalar], in_specs...  2.93 us

profile of v5, /device:TPU:1, one launch (start us, length us, event | category | flops | bytes accessed | tf_op | source)
XLA Modules:
  0.0 70.5 jit_solution(16622213531306437550)
XLA Ops:
  1.3 66.1 %contrast.1 = (f32[128,1280]{1,0:T(8,128)}, f32[128,1280]{1,0:T(8,128)}, f32[16,128]{1,0:T(8,128)}) custom-call(f32[1]{0:T(128)S(6)} %copy.8.ls_ref, s32[16]{0:T(128)} %pairing_in.1, bf16[128,1280]{1,0:T(8,128)(2,1)} %img_in.3, bf16[128,1280]{1,0:T(8,128)(2,1)} %txt_in.3), custom_call_target="tpu_custom_call" | custom-call | tf_op jit(solution)/shard_map/contrast/pallas_call | solution.py:565
  67.4 2.9 %back_norm.1 = (f32[128,1280]{1,0:T(8,128)}, f32[128,1280]{1,0:T(8,128)}, f32[1]{0:T(128)}, f32[1]{0:T(128)}) custom-call(f32[16,128]{1,0:T(8,128)} %get-tuple-element.7.sums, bf16[128,1280]{1,0:T(8,128)(2,1)} %img_in.3, bf16[128,1280]{1,0:T(8,128)(2,1)} %txt_in.3, f32[128,1280]{1,0:T(8,128)} %get-tuple-element.8.gi_in, f32[128,1280]{1,0:T(8,128)} %get-tuple-element.9.gt_in), custom_call_target="tpu_custom_call" | custom-call | tf_op jit(solution)/shard_map/back_norm/pallas_call | solution.py:608

commit v6 on v5

--- a/solution.py
+++ b/solution.py
@@ -224,9 +224,9 @@
     me = device(x, y, z, c)
     sibling = device(x, y, z, 1 - c)
     img_peers = [
-        (dx, dy, dc) for dy in range(2) for dx in range(4) for dc in range(2) if (dx, dy, dc) != (0, 0, 0)
+        (dx, dy, dc) for dy in (1, 0) for dx in (2, 1, 3, 0) for dc in (1, 0) if (dx, dy, dc) != (0, 0, 0)
     ]
-    txt_peers = [(dz, dy) for dy in range(2) for dz in range(4) if (dz, dy) != (0, 0)]
+    txt_peers = [(dz, dy) for dy in (1, 0) for dz in (2, 1, 3, 0) if (dz, dy) != (0, 0)]
 
     def img_peer(dx, dy, dc):
         return device(turn(x, dx), yp if dy else y, z, 1 - c if dc else c)
@@ -376,15 +376,17 @@
         return flip(yb, dy) * 8 + turn(x, dx) * 2 + flip(c, dc)
 
     rows_all[img_me] = jnp.concatenate([jnp.sum(rowacc[p], axis=0, keepdims=True) for p in range(8)], axis=0)
-    k_rows = msgs.take(len(img_peers))
-    for i, p in enumerate(img_peers):
-        msgs.start(k_rows + i, rows_all.at[img_me], rows_all.at[img_me], img_peer(*p))
     cols_all[txt_me] = jnp.concatenate(
         [jnp.sum(colacc[s].T, axis=0, keepdims=True) for s in range(8)], axis=0
     )
-    k_cols = msgs.take(len(txt_peers))
-    for i, p in enumerate(txt_peers):
-        msgs.start(k_cols + i, cols_all.at[txt_me], cols_all.at[txt_me], txt_peer(*p))
+    k_rows, k_cols = msgs.take(len(img_peers)), msgs.take(len(txt_peers))
+    for far in (1, 0):
+        for i, p in enumerate(txt_peers):
+            if p[1] == far:
+                msgs.start(k_cols + i, cols_all.at[txt_me], cols_all.at[txt_me], txt_peer(*p))
+        for i, p in enumerate(img_peers):
+            if p[1] == far:
+                msgs.start(k_rows + i, rows_all.at[img_me], rows_all.at[img_me], img_peer(*p))
 
     def collect_img(first, ref):
         for i, (dx, dy, dc) in enumerate(img_peers):
@@ -500,9 +502,9 @@
         red_t.step(i)
 
     gradient(REDUCE[0], 0)
+    img_product(0)
     for place in REDUCE[1:]:
         tile(pair_of(*place), slot_of(2, 1), place[1] if place[0] == 0 else None)
-    img_product(0)
     txt_product(0)
     for place in REDUCE[1:]:
         gradient(place)
@@ -535,7 +537,7 @@
     for low, ks in ((64, (7, 14, 16)), (0, (13, 15, 12))):
         for n, (r, out) in enumerate(((red_i, gi_out), (red_t, gt_out))):
             part = pl.ds(low, 64)
-            units[n, part] = r.total(low, *ks)
+            units[n, part] = r.total(low, *ks).astype(bf16)
             copy = pltpu.make_async_copy(units.at[n, part], out.at[part], own_sem.at[3 + len(out_copies)])
             copy.start()
             out_copies.append(copy)
@@ -547,7 +549,7 @@
 def epilogue(sums, img_in, txt_in, gi_in, gt_in, gi_out, gt_out, loss_out, gls_out):
     for embed, grad, out in ((img_in, gi_in, gi_out), (txt_in, gt_in, gt_out)):
         inverse, unit = normalize(embed[...])
-        grad_unit = grad[...]
+        grad_unit = grad[...].astype(f32)
         inner = jnp.sum(unit * grad_unit, axis=1, keepdims=True)
         out[...] = inverse * (grad_unit - unit * inner)
     loss_out[0] = jnp.sum(sums[:8]) * (1.0 / (2.0 * BATCH))
@@ -560,11 +562,11 @@
 def local(image_embed, text_embed, log_scale, pairing):
     vmem, smem = pltpu.VMEM, pltpu.SMEM
     in_hbm, in_vmem, in_smem = (pl.BlockSpec(memory_space=m) for m in (pltpu.HBM, vmem, smem))
-    grad = jax.ShapeDtypeStruct((ROWS, D), f32)
+    grad, unit = jax.ShapeDtypeStruct((ROWS, D), f32), jax.ShapeDtypeStruct((ROWS, D), bf16)
     scalar = jax.ShapeDtypeStruct((1,), f32)
     unit_img, unit_txt, sums = pl.pallas_call(
         kernel,
-        out_shape=[grad, grad, jax.ShapeDtypeStruct((16, ROWS), f32)],
+        out_shape=[unit, unit, jax.ShapeDtypeStruct((16, ROWS), f32)],
         in_specs=[in_smem] + [in_hbm] * 3,
         out_specs=[in_hbm] * 3,
         scratch_shapes=[
@@ -594,7 +596,7 @@
             vmem((LAND, D), bf16),
             smem((16,), jnp.int32),
             vmem((2, ROWS, D), bf16),
-            vmem((2, ROWS, D), f32),
+            vmem((2, ROWS, D), bf16),
             vmem((16, ROWS), f32),
             pltpu.SemaphoreType.DMA((8,)),
             pltpu.SemaphoreType.DMA((N_MSG,)),

time: 70.7 us -> 69.9 us (0.989)
  Pallas kernels: 69 us -> 68.2 us
where the time goes in v6:
time: 69.9 us; the launch traced here: 69.7 us
  Pallas kernels  68.2 us (98%)
  between operations  1.47 us (2%)
    pallas_call x1, Pallas kernels, local(): pl.pallas_call(kernel, out_shape=[unit, unit, jax.ShapeDtypeStruct((16, R...  65.5 us
    pallas_call x1, Pallas kernels, local(): pl.pallas_call(epilogue, out_shape=[grad, grad, scalar, scalar], in_specs...  2.75 us

profile of v6, /device:TPU:1, one launch (start us, length us, event | category | flops | bytes accessed | tf_op | source)
XLA Modules:
  0.0 69.7 jit_solution(5533005167257976276)
XLA Ops:
  1.3 65.5 %contrast.1 = (bf16[128,1280]{1,0:T(8,128)(2,1)}, bf16[128,1280]{1,0:T(8,128)(2,1)}, f32[16,128]{1,0:T(8,128)}) custom-call(f32[1]{0:T(128)S(6)} %copy.8.ls_ref, s32[16]{0:T(128)} %pairing_in.1, bf16[128,1280]{1,0:T(8,128)(2,1)} %img_in.3, bf16[128,1280]{1,0:T(8,128)(2,1)} %txt_in.3), custom_call_target="tpu_custom_call" | custom-call | tf_op jit(solution)/shard_map/contrast/pallas_call | solution.py:567
  66.8 2.8 %back_norm.1 = (f32[128,1280]{1,0:T(8,128)}, f32[128,1280]{1,0:T(8,128)}, f32[1]{0:T(128)}, f32[1]{0:T(128)}) custom-call(f32[16,128]{1,0:T(8,128)} %get-tuple-element.7.sums, bf16[128,1280]{1,0:T(8,128)(2,1)} %img_in.3, bf16[128,1280]{1,0:T(8,128)(2,1)} %txt_in.3, bf16[128,1280]{1,0:T(8,128)(2,1)} %get-tuple-element.8.gi_in, ...), custom_call_target="tpu_custom_call" | custom-call | tf_op jit(solution)/shard_map/back_norm/pallas_call | solution.py:610
